TPU v7x, 32 devices: a whole 2x2x4 slice. The times are simulated.
32 devices in a mesh: utt: 4 (over y, core), seq: 8 (over z, x).
Axes of the slice: x: 2, y: 2, z: 4, core: 2. Of those that a mesh axis runs over, the one named last changes fastest.
Arguments:
- frames: float32 [8, 1024, 512], P('utt', 'seq'), may hold values from -6 to 6
- lengths: int32 [8], P('utt'), may hold values from 256 to 1024, as said below
- out_grad: float32 [8, 1024, 512], P('utt', 'seq'), may hold values from -6 to 6
- norm_gain: bfloat16 [5, 512], replicated, may hold values from 0.5 to 1.5
- norm_bias: bfloat16 [5, 512], replicated, may hold values from -1 to 1
- feed_in: bfloat16 [2, 512, 2048], replicated, may hold values from -0.25 to 0.25
- feed_in_bias: bfloat16 [2, 2048], replicated, may hold values from -1 to 1
- feed_out: bfloat16 [2, 2048, 512], replicated, may hold values from -0.125 to 0.125
- feed_out_bias: bfloat16 [2, 512], replicated, may hold values from -1 to 1
- attend_in: bfloat16 [4, 512, 512], replicated, may hold values from -0.25 to 0.25
- attend_vectors: bfloat16 [5, 512], replicated, may hold values from -1.5 to 1.5
- attend_out: bfloat16 [512, 512], replicated, may hold values from -1 to 1
- mixer_in: bfloat16 [512, 1024], replicated, may hold values from -0.25 to 0.25
- mixer_in_bias: bfloat16 [1024], replicated, may hold values from -1 to 1
- depthwise: bfloat16 [512, 9], replicated, may hold values from -2 to 2
- mixer_vectors: bfloat16 [2, 512], replicated, may hold values from -1 to 1
- mixer_out: bfloat16 [512, 512], replicated, may hold values from -0.25 to 0.25
- batch_gain: bfloat16 [512], replicated, may hold values from 0.5 to 1.5
- batch_shift: bfloat16 [512], replicated, may hold values from -1 to 1
- running_mean: float32 [512], replicated, may hold values from -0.08 to 0.08
- running_variance: float32 [512], replicated, may hold values from 0.004 to 0.04
Outputs:
- layer_output: float32 [8, 1024, 512], P('utt', 'seq')
- frames_grad: float32 [8, 1024, 512], P('utt', 'seq')
- norm_gain_grad: float32 [5, 512], replicated
- norm_bias_grad: float32 [5, 512], replicated
- feed_in_grad: float32 [2, 512, 2048], replicated
- feed_in_bias_grad: float32 [2, 2048], replicated
- feed_out_grad: float32 [2, 2048, 512], replicated
- feed_out_bias_grad: float32 [2, 512], replicated
- attend_in_grad: float32 [4, 512, 512], replicated
- attend_vectors_grad: float32 [5, 512], replicated
- attend_out_grad: float32 [512, 512], replicated
- mixer_in_grad: float32 [512, 1024], replicated
- mixer_in_bias_grad: float32 [1024], replicated
- depthwise_grad: float32 [512, 9], replicated
- mixer_vectors_grad: float32 [2, 512], replicated
- mixer_out_grad: float32 [512, 512], replicated
- batch_gain_grad: float32 [512], replicated
- batch_shift_grad: float32 [512], replicated
- new_mean: float32 [512], replicated
- new_variance: float32 [512], replicated
Inputs may be any that keep to these rules, and one draw needn't show every extreme that they name: `lengths`: in each aligned block of 2 utterances (those of one index of utt) at least one has exactly 1024 frames.
All inputs are finite; a program needn't handle non-finite values.
Results may differ from a plain program's by a relative error of at most 0.025.
Values may be sent and summed in bfloat16 or wider, within the bound.
No kernel may reach another device: no remote copies, remote signals or barrier semaphores. Data moves between devices by JAX's collectives and lax.ppermute only.
A program may use at most 320 MiB of HBM per device.

v0:
```python
import functools
import math

import jax
import jax.numpy as jnp
import numpy as np
from jax import lax
from jax.experimental import pallas as pl
from jax.experimental.pallas import tpu as pltpu
from jax.sharding import PartitionSpec as P

HEADS = 8
KERNEL = 9
HEAD_DIM = 64


TOP_PRECISION = lax.Precision.HIGHEST
EPSILON = 1e-05
VMEM_LIMIT = 63 * 1024 * 1024
SUM_LIMIT = 20 * 1024 * 1024
FOLD_LIMIT = SUM_LIMIT
HALO = 8


def wide(values):
    return values.astype(jnp.float32)


def low(values):
    return values.astype(jnp.bfloat16)


def matmul(first_operand, second_operand):
    return jnp.dot(first_operand, second_operand, preferred_element_type=jnp.float32)


def column_sum(values):
    return jnp.sum(wide(values), axis=0, keepdims=True)


def normalize(values):
    average = jnp.mean(values, axis=-1, keepdims=True)
    centered = values - average
    spread = jnp.mean(centered * centered, axis=-1, keepdims=True)
    inverse = lax.rsqrt(spread + EPSILON)
    return centered * inverse, inverse


def scaled_norm(normed, gains, biases, number):
    return normed * wide(gains[number : number + 1, :]) + wide(biases[number : number + 1, :])


def norm_back(grad_rows, normed, inverse, gains, number, own=lambda values: values):
    scaled = grad_rows * wide(gains[number : number + 1, :])
    inner = (
        scaled
        - jnp.mean(scaled, axis=-1, keepdims=True)
        - normed * jnp.mean(scaled * normed, axis=-1, keepdims=True)
    )
    return inner * inverse, column_sum(own(grad_rows * normed)), column_sum(own(grad_rows))


def logistic(values):
    return 1.0 / (1.0 + jnp.exp(-values))


def silu_slope(preact, sigmoid):
    return sigmoid * (1.0 + preact * (1.0 - sigmoid))


def frame_places(info, rows, utterances, halo):
    per = rows // utterances
    row = lax.broadcasted_iota(jnp.int32, (rows, 1), 0)
    limit = jnp.full((rows, 1), info[utterances], jnp.int32)
    for utterance in range(utterances - 1):
        limit = jnp.where(row // per == utterance, info[1 + utterance], limit)
    return info[0] - halo + row % per, limit


def flags(condition):
    return jnp.where(condition, 1.0, 0.0)


def own_rows(values, utterances):
    per = values.shape[0] // utterances
    return jnp.concatenate(
        [values[u * per + HALO : (u + 1) * per - HALO] for u in range(utterances)], axis=0
    )


def with_sides(values, sides, utterances):
    per = values.shape[0] // utterances
    pieces = []
    for u in range(utterances):
        pieces.append(sides[2 * u * HALO : (2 * u + 1) * HALO])
        pieces.append(values[u * per : (u + 1) * per])
        pieces.append(sides[(2 * u + 1) * HALO : (2 * u + 2) * HALO])
    return jnp.concatenate(pieces, axis=0)


def blocks_of_heads(rows, utterances):
    per = rows.shape[0] // utterances
    first = lax.broadcasted_iota(jnp.int32, (per, 2 * HEAD_DIM), 1) < HEAD_DIM
    blocks = []
    for pair in range(HEADS // 2):
        columns = rows[:, pair * 2 * HEAD_DIM : (pair + 1) * 2 * HEAD_DIM]
        top, bottom = columns[:per], columns[per:]
        blocks.append(jnp.where(first, top, pltpu.roll(bottom, HEAD_DIM, 1)))
        blocks.append(jnp.where(first, pltpu.roll(top, HEAD_DIM, 1), bottom))
    return blocks


def rows_of_heads(blocks):
    per = blocks[0].shape[0]
    first = lax.broadcasted_iota(jnp.int32, (per, 2 * HEAD_DIM), 1) < HEAD_DIM
    columns = []
    for pair in range(HEADS // 2):
        left, right = blocks[2 * pair], blocks[2 * pair + 1]
        top = jnp.where(first, left, pltpu.roll(right, HEAD_DIM, 1))
        bottom = jnp.where(first, pltpu.roll(left, HEAD_DIM, 1), right)
        columns.append(jnp.concatenate([top, bottom], axis=0))
    return jnp.concatenate(columns, axis=1)


def whole_array(shape):
    return pl.BlockSpec(shape, lambda i: (0,) * len(shape))


class Part:
    def __init__(self, array, block, index):
        self.array, self.block, self.index = array, block, index

    def spec(self):
        def index(i, *numbers):
            return tuple(at(*numbers) if callable(at) else at for at in self.index)

        return pl.BlockSpec(self.block, index)


def vmem_call(kernel, shapes, smem, operands, scratch=(), cost=0, held=(), numbers=()):
    def whole(shape):
        return pl.BlockSpec(shape, lambda i, *numbers: (0,) * len(shape))

    return pl.pallas_call(
        kernel,
        grid_spec=pltpu.PrefetchScalarGridSpec(
            num_scalar_prefetch=len(numbers),
            grid=(1,),
            in_specs=[pl.BlockSpec(memory_space=pltpu.SMEM)] * len(smem)
            + [
                operand.spec() if isinstance(operand, Part) else whole(operand.shape)
                for operand in operands
            ]
            + [pl.BlockSpec(memory_space=pl.ANY)] * len(held),
            out_specs=[whole(shape) for shape, _ in shapes],
            scratch_shapes=list(scratch),
        ),
        out_shape=[jax.ShapeDtypeStruct(shape, dtype) for shape, dtype in shapes],
        compiler_params=pltpu.CompilerParams(vmem_limit_bytes=VMEM_LIMIT),
        cost_estimate=pl.CostEstimate(flops=cost, bytes_accessed=cost // 300, transcendentals=0),
    )(
        *numbers,
        *smem,
        *(operand.array if isinstance(operand, Part) else operand for operand in operands),
        *held,
    )


def fetch(pairs, semaphores):
    copies = [
        pltpu.make_async_copy(source, target, semaphores.at[number])
        for number, (source, target) in enumerate(pairs)
    ]
    for copy in copies:
        copy.start()
    return copies


def feed_rows(values, gains, biases, copies, weight_in, bias_in, weight_out, bias_out):
    normed, _ = normalize(values)
    hidden = low(scaled_norm(normed, gains, biases, 0))
    copies[0].wait()
    preact = matmul(hidden, weight_in[...]) + wide(bias_in[0:1, :])
    sigmoid = logistic(preact)
    active = low(preact * sigmoid)
    copies[1].wait()
    branch = matmul(active, weight_out[...]) + wide(bias_out[0:1, :])
    return values + 0.5 * branch, preact, sigmoid, active


def entry_kernel(
    utterances,
    frames,
    gains,
    biases,
    bias_in,
    bias_out,
    vectors,
    grads_head,
    grads_tail,
    feed_in,
    feed_out,
    attend_in,
    head_out,
    tail_out,
    after_out,
    slope_out,
    pack_out,
    sent_out,
    weight_in,
    weight_out,
    weight_attend,
    semaphores,
):
    copies = fetch(
        [
            (feed_in.at[0], weight_in),
            (feed_out.at[0], weight_out),
            (attend_in.at[pl.ds(0, 3)], weight_attend),
        ],
        semaphores,
    )
    per = frames.shape[0] // utterances
    for u in range(utterances):
        head_out[u, 0:HALO, :] = frames[u * per : u * per + HALO, :]
        head_out[u, HALO:, :] = grads_head[u]
        tail_out[u, 0:HALO, :] = frames[(u + 1) * per - HALO : (u + 1) * per, :]
        tail_out[u, HALO:, :] = grads_tail[u]
    units, features = slope_out.shape[1], frames.shape[1]
    pack_out[:, units : units + features] = low(scaled_norm(normalize(frames[...])[0], gains, biases, 0))
    after, preact, sigmoid, active = feed_rows(
        frames[...], gains, biases, copies, weight_in, bias_in, weight_out, bias_out
    )
    slope_out[...] = low(silu_slope(preact, sigmoid))
    pack_out[:, :units] = active
    after_out[...] = after
    normed, _ = normalize(after)
    hidden = low(scaled_norm(normed, gains, biases, 1))
    pack_out[:, units + features :] = hidden
    copies[2].wait()
    queries = matmul(hidden, weight_attend[0]) + wide(vectors[0:1, :])
    parts = (
        queries + wide(vectors[3:4, :]),
        matmul(hidden, weight_attend[1]),
        matmul(hidden, weight_attend[2]) + wide(vectors[1:2, :]),
    )
    lanes = 2 * HEAD_DIM
    for number, part in enumerate(parts):
        for head, block in enumerate(blocks_of_heads(part, utterances)):
            sent_out[head, :, number * lanes : (number + 1) * lanes] = low(block)


def sides_kernel(
    before,
    behind,
    gains,
    biases,
    bias_in,
    bias_out,
    feed_in,
    feed_out,
    after_out,
    grads_out,
    weight_in,
    weight_out,
    semaphores,
):
    copies = fetch([(feed_in.at[0], weight_in), (feed_out.at[0], weight_out)], semaphores)
    frames, grads = (
        jnp.concatenate(
            [
                source[u, first : first + HALO, :]
                for u in range(before.shape[0])
                for source in (before, behind)
            ],
            axis=0,
        )
        for first in (0, HALO)
    )
    grads_out[...] = grads
    after_out[...] = feed_rows(
        frames, gains, biases, copies, weight_in, bias_in, weight_out, bias_out
    )[0]


def mixer_kernel(
    utterances,
    info,
    blocks,
    after,
    after_sides,
    gains,
    biases,
    attend_out,
    vectors,
    mixer_in,
    mixer_bias,
    taps,
    mixer_vectors,
    after_out,
    pack_out,
    linear_out,
    gate_out,
    gated_out,
    convolved_out,
    sums_out,
    padded,
):
    per = after.shape[0] // utterances
    main, before, behind = [], [], []
    for head in range(HEADS):
        block = wide(blocks[head])
        main.append(block[:per])
        before.append(block[per : per + HALO])
        behind.append(block[per + HALO :])
    attended = rows_of_heads(main)
    features = after.shape[1]
    pack_out[:, :features] = low(attended)
    before, behind = rows_of_heads(before), rows_of_heads(behind)
    sides = []
    for u in range(utterances):
        sides += [before[u * HALO : (u + 1) * HALO], behind[u * HALO : (u + 1) * HALO]]
    attended = low(with_sides(attended, jnp.concatenate(sides, axis=0), utterances))
    values = with_sides(after[...], after_sides[...], utterances)
    values = values + matmul(attended, attend_out[...]) + wide(vectors[2:3, :])
    after_out[...] = values
    normed, _ = normalize(values)
    scaled = scaled_norm(normed, gains, biases, 2)
    pack_out[:, features:] = low(own_rows(scaled, utterances))
    preact = matmul(low(scaled), mixer_in[...])
    preact = preact + wide(mixer_bias[...])
    rows = values.shape[0]
    linear = preact[:, :features]
    gate = logistic(preact[:, features:])
    linear_out[...] = own_rows(linear, utterances)
    gate_out[...] = own_rows(gate, utterances)
    place, limit = frame_places(info, rows, utterances, HALO)
    mask = flags((place >= 0) & (place < limit))
    gated = low(linear * gate * mask)
    gated_out[...] = gated
    fill_padded(padded, wide(gated), utterances)
    total = None
    for offset in range(KERNEL):
        term = wide(taps[offset : offset + 1, :]) * moved(
            padded, utterances, offset - KERNEL // 2, rows // utterances
        )
        total = term if total is None else total + term
    convolved = total + wide(mixer_vectors[0:1, :])
    convolved_out[...] = convolved
    mask = own_rows(mask, utterances)
    convolved = own_rows(convolved, utterances)
    count = jnp.sum(mask, axis=0, keepdims=True)
    local_sum = jnp.sum(convolved * mask, axis=0, keepdims=True)
    centered = (convolved - local_sum / jnp.maximum(count, 1.0)) * mask
    share(sums_out, local_sum, jnp.sum(centered * centered, axis=0, keepdims=True))


def fill_padded(padded, values, utterances):
    per = values.shape[0] // utterances
    zeros = jnp.zeros((8, values.shape[1]), jnp.float32)
    for u in range(utterances):
        padded[u, 0:8, :] = zeros
        padded[u, 8 : 8 + per, :] = values[u * per : (u + 1) * per, :]
        padded[u, 8 + per : 16 + per, :] = zeros


def moved(padded, utterances, start, per, first=0):
    return jnp.concatenate(
        [
            padded[u, 8 + first + start : 8 + first + start + per, :]
            for u in range(utterances)
        ],
        axis=0,
    )


def share(sums_out, *rows):
    tile = jnp.concatenate(
        [row[:, i : i + 128] for row in rows for i in range(0, row.shape[1], 128)], axis=0
    )
    for copy in range(sums_out.shape[0] // 8):
        sums_out[copy * 8 : copy * 8 + 8, :] = tile


def as_row(tile):
    return jnp.concatenate([tile[i : i + 1] for i in range(tile.shape[0])], axis=1)


def frame_counts(limits, shape, utterances, seq_count, per):
    place = lax.broadcasted_iota(jnp.int32, shape, 0)
    owner, first = place // seq_count, place % seq_count * per
    total = jnp.zeros(shape, jnp.int32)
    for number in range(limits.shape[0]):
        inside = jnp.clip(limits[number] - first, 0, per)
        total = total + jnp.where(owner == number // utterances, inside, 0)
    return total.astype(jnp.float32)


def middle_kernel(
    utterances,
    seq_count,
    limits,
    convolved,
    shared,
    after,
    grads,
    grad_sides,
    gains,
    biases,
    batch_gain,
    batch_shift,
    running_mean,
    running_variance,
    mixer_out,
    vectors,
    bias_in,
    bias_out,
    feed_in,
    feed_out,
    layer_out,
    grad_mixer_out,
    grad_batch_out,
    normed_out,
    pack_out,
    sums_out,
    batch_out_rows,
    vector_out,
    weight_in,
    weight_out,
    semaphores,
):
    def own(values):
        return own_rows(values, utterances)

    features, units = feed_in.shape[1:]

    def pack(number, rows):
        first = 2 * units + number * features
        pack_out[:, first : first + features] = rows

    copies = fetch([(feed_in.at[1], weight_in), (feed_out.at[1], weight_out)], semaphores)
    parts = shared[...].reshape(-1, 8, 128)
    per = grads.shape[0] // utterances
    counts = frame_counts(limits, parts.shape, utterances, seq_count, per)
    totals = jnp.sum(parts, axis=0)
    valid_tile = jnp.sum(counts, axis=0)
    valid = as_row(valid_tile[:4])
    average_tile = totals / valid_tile
    drift = parts / jnp.maximum(counts, 1.0) - average_tile
    spreads = jnp.sum(counts * drift * drift, axis=0)
    average = as_row(average_tile[:4])
    variance = as_row((totals[4:] + spreads[:4]) / valid_tile[:4])
    inverse_batch = lax.rsqrt(variance + EPSILON)
    batch_out_rows[0:1, :] = inverse_batch
    batch_out_rows[1:2, :] = valid
    batch_out_rows[2:3, :] = 0.9 * running_mean[...] + 0.1 * average
    batch_out_rows[3:4, :] = 0.9 * running_variance[...] + 0.1 * variance * valid / (valid - 1.0)
    normed_batch = (convolved[...] - average) * inverse_batch
    normed_out[...] = normed_batch
    batch = normed_batch * wide(batch_gain[...]) + wide(batch_shift[...])
    batch_sigmoid = logistic(batch)
    swished = low(batch * batch_sigmoid)
    pack(2, low(own(batch * batch_sigmoid)))
    values = after[...] + matmul(swished, mixer_out[...]) + wide(vectors[1:2, :])
    normed, inverse = normalize(values)
    scaled = scaled_norm(normed, gains, biases, 3)
    pack(0, low(own(scaled)))
    copies[0].wait()
    preact = matmul(low(scaled), weight_in[...]) + wide(bias_in[1:2, :])
    sigmoid = logistic(preact)
    activated = preact * sigmoid
    active = low(activated)
    pack_out[:, units : 2 * units] = low(own(activated))
    copies[1].wait()
    branch = matmul(active, weight_out[...]) + wide(bias_out[1:2, :])
    normed_last, inverse_last = normalize(values + 0.5 * branch)
    layer_out[...] = own(scaled_norm(normed_last, gains, biases, 4))
    grad_second, gain_last, shift_last = norm_back(
        with_sides(grads[...], grad_sides[...], utterances),
        normed_last,
        inverse_last,
        gains,
        4,
        own,
    )
    grad_low = low(0.5 * grad_second)
    grad_low_own = low(own(0.5 * grad_second))
    pack(1, grad_low_own)
    grad_pre = rows_dot(grad_low, weight_out[...]) * silu_slope(preact, sigmoid)
    grad_pre_own = low(own(grad_pre))
    pack_out[:, :units] = grad_pre_own
    grad_values, gain_three, shift_three = norm_back(
        rows_dot(low(grad_pre), weight_in[...]), normed, inverse, gains, 3, own
    )
    grad_mixer = grad_second + grad_values
    grad_mixer_own = own(grad_mixer)
    grad_mixer_out[...] = grad_mixer_own
    branch_own = low(grad_mixer_own)
    pack(3, branch_own)
    grad_batch = rows_dot(low(grad_mixer), mixer_out[...]) * silu_slope(batch, batch_sigmoid)
    grad_batch_out[...] = grad_batch
    share(sums_out, column_sum(own(grad_batch)), column_sum(own(grad_batch * normed_batch)))
    bias_sum = column_sum(grad_pre_own)
    put_rows(
        vector_out,
        [gain_last, shift_last, gain_three, shift_three]
        + [bias_sum[:, i : i + features] for i in range(0, bias_sum.shape[1], features)]
        + [column_sum(grad_low_own), column_sum(branch_own)],
    )


def put_rows(out, rows):
    for number, row in enumerate(rows):
        out[number : number + 1, :] = row
    out[len(rows) :, :] = jnp.zeros((out.shape[0] - len(rows), out.shape[1]), jnp.float32)


def mixer_back_kernel(
    utterances,
    info,
    grad_batch,
    normed_batch,
    shared,
    batch_rows,
    batch_gain,
    gated,
    linear,
    gate,
    grad_mixer,
    after,
    gains,
    taps,
    mixer_in,
    attend_out,
    batch_grads_out,
    grad_attend_out,
    pack_out,
    sent_out,
    vector_out,
    padded,
    gated_padded,
):
    totals = jnp.sum(shared[...].reshape(-1, 8, 128), axis=0)
    shift_grad, gain_grad = as_row(totals[:4]), as_row(totals[4:])
    batch_grads_out[0:1, :] = shift_grad
    batch_grads_out[1:2, :] = gain_grad
    rows, features = grad_batch.shape
    place, limit = frame_places(info, rows, utterances, HALO)
    mask = flags((place >= 0) & (place < limit))
    inside = flags((place >= 0) & (place < info[utterances + 1]))
    inverse_batch, valid = batch_rows[0:1, :], batch_rows[1:2, :]
    grad_conv = low(
        inside
        * wide(batch_gain[...])
        * inverse_batch
        * (grad_batch[...] - mask / valid * (shift_grad + normed_batch[...] * gain_grad))
    )
    conv_wide = wide(grad_conv)
    fill_padded(padded, conv_wide, utterances)
    fill_padded(gated_padded, wide(gated[...]), utterances)
    conv_own = own_rows(conv_wide, utterances)
    per = rows // utterances - 2 * HALO
    margin = KERNEL // 2
    total = None
    tap_rows = []
    for offset in range(KERNEL):
        term = wide(taps[offset : offset + 1, :]) * moved(
            padded, utterances, margin - offset, per, HALO
        )
        total = term if total is None else total + term
        near = moved(gated_padded, utterances, offset - margin, per, HALO)
        tap_rows.append(jnp.sum(conv_own * near, axis=0, keepdims=True))
    grad_gated = own_rows(mask, utterances) * total
    gate_half = gate[...]
    grad_pre = low(
        jnp.concatenate(
            [
                grad_gated * gate_half,
                grad_gated * linear[...] * gate_half * (1.0 - gate_half),
            ],
            axis=1,
        )
    )
    pack_out[:, : 2 * features] = grad_pre
    normed, inverse = normalize(own_rows(after[...], utterances))
    grad_values, gain_two, shift_two = norm_back(
        rows_dot(grad_pre, mixer_in[...]), normed, inverse, gains, 2
    )
    grad_attend = grad_mixer[...] + grad_values
    grad_attend_out[...] = grad_attend
    branch = low(grad_attend)
    pack_out[:, 2 * features :] = branch
    grad_attended = rows_dot(branch, attend_out[...])
    for head, block in enumerate(blocks_of_heads(grad_attended, utterances)):
        sent_out[head] = low(block)
    bias_sum = column_sum(grad_pre)
    put_rows(
        vector_out,
        [gain_two, shift_two, column_sum(conv_own), column_sum(branch)]
        + [bias_sum[:, :features], bias_sum[:, features:]]
        + tap_rows,
    )


def entry_back_kernel(
    core,
    returned,
    grad_attend,
    frames,
    after,
    slope,
    gains,
    feed_in,
    feed_out,
    attend_in,
    frames_out,
    pack_out,
    grad_pre_out,
    vector_out,
    weight_in,
    weight_out,
    weight_attend,
    semaphores,
):
    copies = fetch(
        [
            (attend_in.at[pl.ds(0, 3)], weight_attend),
            (feed_out.at[0], weight_out),
            (feed_in.at[0], weight_in),
        ],
        semaphores,
    )
    lanes = 2 * HEAD_DIM
    features, units = feed_in.shape[1:]

    def pack(number, rows):
        first = units // 2 + number * features
        pack_out[:, first : first + features] = rows

    grad_hidden = None
    low_rows = []
    for number in range(3):
        rows = low(
            rows_of_heads(
                [
                    wide(returned[head, :, number * lanes : (number + 1) * lanes])
                    for head in range(HEADS)
                ]
            )
        )
        pack(number, rows)
        low_rows.append(rows)
        if number == 0:
            copies[0].wait()
        term = rows_dot(rows, weight_attend[number])
        grad_hidden = term if grad_hidden is None else grad_hidden + term
    normed, inverse = normalize(after[...])
    grad_values, gain_one, shift_one = norm_back(grad_hidden, normed, inverse, gains, 1)
    grad_first = grad_attend[...] + grad_values
    grad_low = low(0.5 * grad_first)
    pack(3, grad_low)
    copies[1].wait()
    grad_pre = low(rows_dot(grad_low, weight_out[...]) * wide(slope[...]))
    for half in range(2):
        rows = grad_pre[:, half * units // 2 : (half + 1) * units // 2]

        @pl.when(core[0] == half)
        def _():
            grad_pre_out[...] = rows

        @pl.when(core[0] != half)
        def _():
            pack_out[:, : units // 2] = rows

    normed, inverse = normalize(frames[...])
    copies[2].wait()
    grad_values, gain_zero, shift_zero = norm_back(
        rows_dot(grad_pre, weight_in[...]), normed, inverse, gains, 0
    )
    frames_out[...] = grad_first + grad_values
    bias_sum = column_sum(grad_pre)
    put_rows(
        vector_out,
        [gain_zero, shift_zero, gain_one, shift_one]
        + [bias_sum[:, i : i + features] for i in range(0, bias_sum.shape[1], features)]
        + [column_sum(grad_low), column_sum(low_rows[0]), column_sum(low_rows[2])],
    )


def vectors_kernel(
    rows, gain_out, bias_out, in_bias_out, out_bias_out, attend_out, mixer_bias_out, mixer_out, taps_out
):
    middle, mixer, entry, heads = (0, 16, 32, 48)
    features = gain_out.shape[1]

    def take(out, target, start):
        out[target : target + 1, :] = rows[start : start + 1, :]

    for out, first in ((gain_out, 0), (bias_out, 1)):
        take(out, 0, entry + first)
        take(out, 1, entry + 2 + first)
        take(out, 2, mixer + first)
        take(out, 3, middle + 2 + first)
        take(out, 4, middle + first)
    for target, start in ((0, entry + 4), (1, middle + 4)):
        for column in range(4):
            in_bias_out[target : target + 1, column * features : (column + 1) * features] = rows[
                start + column : start + column + 1, :
            ]
    take(out_bias_out, 0, entry + 8)
    take(out_bias_out, 1, middle + 8)
    for target, start in enumerate((entry + 9, entry + 10, mixer + 3, heads, heads + 1)):
        take(attend_out, target, start)
    for column in range(2):
        mixer_bias_out[0:1, column * features : (column + 1) * features] = rows[
            mixer + 4 + column : mixer + 5 + column, :
        ]
    take(mixer_out, 0, mixer + 2)
    take(mixer_out, 1, middle + 9)
    taps_out[...] = rows[mixer + 6 : mixer + 6 + KERNEL, :]


def axis_bits(axis):
    return [(axis, 1 << bit) for bit in range(lax.axis_size(axis).bit_length() - 1)]


def swap(values, step):
    axis, mask = step
    return lax.ppermute(values, axis, [(i, i ^ mask) for i in range(lax.axis_size(axis))])


def side(step):
    axis, mask = step
    return (lax.axis_index(axis) // mask) % 2


def swap_all(stripes, steps):
    return [swap(rows, step) for rows, step in zip(stripes, steps)]


def add_low(first_operand, second_operand):
    total = first_operand.astype(jnp.float32) + second_operand.astype(jnp.float32)
    return total.astype(jnp.bfloat16)


def fold_kernel(stripes, arrays, parts, sides, *refs):
    for number in range(stripes):
        sources = refs[2 * arrays * number : 2 * arrays * (number + 1)]
        for keeping in range(2):
            place = sides[number] if keeping else 1 - sides[number]
            out = refs[2 * arrays * stripes + 2 * number + keeping]
            first = 0
            for array in range(arrays):
                own, other = sources[2 * array : 2 * array + 2]
                height = own.shape[0] // (2 * parts)
                for part in range(parts):
                    start = pl.multiple_of((2 * part + place) * height, 16)
                    rows = pl.ds(start, height)
                    out[first : first + height, :] = add_low(own[rows, :], other[rows, :])
                    first += height


def fold_rows(pairs, steps, parts=1):
    operands = list(zip(*(rows for pair in pairs for rows in pair)))
    heights = [sum(rows.shape[0] for rows in four[::2]) // 2 for four in operands]
    if any(rows.shape[0] // parts % 32 for four in operands for rows in four):
        sent, kept = [], []
        for four, step in zip(operands, steps):
            sums = [add_low(*four[i : i + 2]) for i in range(0, len(four), 2)]
            for place, results in ((1 - side(step), sent), (side(step), kept)):
                pieces = []
                for rows in sums:
                    height = rows.shape[0] // (2 * parts)
                    pieces += [
                        lax.dynamic_slice_in_dim(rows, (2 * part + place) * height, height, 0)
                        for part in range(parts)
                    ]
                results.append(jnp.concatenate(pieces, axis=0))
        return sent, kept

    def whole(rows):
        return pl.BlockSpec((rows, 512), lambda i, sides: (0, 0))

    outs = [height for height in heights for _ in range(2)]
    results = pl.pallas_call(
        functools.partial(fold_kernel, len(steps), len(pairs), parts),
        grid_spec=pltpu.PrefetchScalarGridSpec(
            num_scalar_prefetch=1,
            grid=(1,),
            in_specs=[whole(rows.shape[0]) for four in operands for rows in four],
            out_specs=[whole(height) for height in outs],
        ),
        out_shape=[jax.ShapeDtypeStruct((height, 512), jnp.bfloat16) for height in outs],
        compiler_params=pltpu.CompilerParams(vmem_limit_bytes=FOLD_LIMIT),
        cost_estimate=pl.CostEstimate(
            flops=0, bytes_accessed=6 * 1024 * sum(outs), transcendentals=0
        ),
    )(jnp.stack([side(step) for step in steps]), *(rows for four in operands for rows in four))
    return list(results[::2]), list(results[1::2])


def add_kernel(stripes, *refs):
    for number in range(stripes):
        refs[2 * stripes + number][...] = add_low(refs[2 * number][...], refs[2 * number + 1][...])


def add_rows(kept, arrived):
    if any(rows.shape[0] % 16 for rows in kept):
        return [add_low(*pair) for pair in zip(kept, arrived)]
    specs = [whole_array(rows.shape) for rows in kept]
    return list(
        pl.pallas_call(
            functools.partial(add_kernel, len(kept)),
            grid=(1,),
            in_specs=[spec for spec in specs for _ in range(2)],
            out_specs=specs,
            out_shape=[jax.ShapeDtypeStruct(rows.shape, rows.dtype) for rows in kept],
            compiler_params=pltpu.CompilerParams(vmem_limit_bytes=SUM_LIMIT),
        )(*(rows for pair in zip(kept, arrived) for rows in pair))
    )


def join_kernel(stripes, sides, *refs):
    for number in range(stripes):
        own, other, out = refs[2 * number], refs[2 * number + 1], refs[2 * stripes + number]
        height = own.shape[0] // 2
        for part in range(2):
            for source, place in ((own, sides[number]), (other, 1 - sides[number])):
                start = pl.multiple_of((2 * part + place) * height, 16)
                out[pl.ds(start, height), :] = source[part * height : (part + 1) * height, :]


def join_rows(stripes, arrived, steps):
    heights = [rows.shape[0] // 2 for rows in stripes]
    if any(height % 16 for height in heights):
        joined = []
        for rows, other, step, height in zip(stripes, arrived, steps, heights):
            first = side(step) == 0
            low_rows, high_rows = jnp.where(first, rows, other), jnp.where(first, other, rows)
            joined.append(
                jnp.concatenate(
                    [
                        half[part]
                        for part in (slice(0, height), slice(height, None))
                        for half in (low_rows, high_rows)
                    ],
                    axis=0,
                )
            )
        return joined

    def whole(height):
        return pl.BlockSpec((height, 512), lambda i, sides: (0, 0))

    return list(
        pl.pallas_call(
            functools.partial(join_kernel, len(stripes)),
            grid_spec=pltpu.PrefetchScalarGridSpec(
                num_scalar_prefetch=1,
                grid=(1,),
                in_specs=[whole(2 * height) for height in heights for _ in range(2)],
                out_specs=[whole(4 * height) for height in heights],
            ),
            out_shape=[jax.ShapeDtypeStruct((4 * height, 512), jnp.bfloat16) for height in heights],
            compiler_params=pltpu.CompilerParams(vmem_limit_bytes=SUM_LIMIT),
            cost_estimate=pl.CostEstimate(
                flops=0, bytes_accessed=8 * 1024 * sum(heights), transcendentals=0
            ),
        )(
            jnp.stack([side(step) for step in steps]),
            *(rows for pair in zip(stripes, arrived) for rows in pair),
        )
    )


def tie(*groups):
    return lax.optimization_barrier(groups)


def step_orders():
    utt, seq = axis_bits("utt"), axis_bits("seq")
    across, line, rest = utt[1:], seq[:1], seq[1:]
    return (
        line + across + rest,
        across + rest + line,
        rest[:1] + line + across + rest[1:],
    )


def all_shared(copies):
    return lax.all_to_all(copies, ("utt", "seq"), 0, 0, tiled=True)


def from_neighbours(head, tail):
    count = lax.axis_size("seq")
    before = lax.ppermute(tail, "seq", [(i, i + 1) for i in range(count - 1)])
    behind = lax.ppermute(head, "seq", [(i + 1, i) for i in range(count - 1)])
    return before, behind


def pair_rows(mine, theirs, start=0, width=None):
    columns = slice(start, start + (width or mine.shape[1]))
    return jnp.concatenate([mine[:, columns], theirs[:, columns]], axis=0)


def outer(left, right):
    return low(matmul(left.T, right))


def put_half(outs, side_number, half, value):
    @pl.when(side_number == half)
    def _():
        outs[1][...] = value

    @pl.when(side_number != half)
    def _():
        outs[0][...] = value


def feed_blocks(refs, outs, sides):
    hidden, grad_pre, active, grad_low = (refs[2 * i : 2 * i + 2] for i in range(4))
    hidden_cols = pair_rows(*hidden).T
    grad_rows = pair_rows(*grad_low)
    for half in range(2):
        block = low(matmul(hidden_cols, pair_rows(*grad_pre, 512 * half, 512)))
        put_half(outs[:2], sides[1], half, block)
        block = outer(pair_rows(*active, 512 * half, 512), grad_rows)
        put_half(outs[2:4], sides[2], half, block)


def second_kernel(places, *refs):
    feed_blocks(refs[:8], refs[8:], places)


def mixer_blocks_kernel(places, *refs):
    refs, outs = refs[:12], refs[12:]
    mixer = outer(pair_rows(*refs[:2]), pair_rows(*refs[2:4]))
    branch = outer(pair_rows(*refs[4:6]), pair_rows(*refs[6:8]))
    attend = outer(pair_rows(*refs[8:10]), pair_rows(*refs[10:12]))
    for half in range(2):
        pieces = (
            mixer[256 * half : 256 * half + 256],
            branch[128 * half : 128 * half + 128],
            attend[128 * half : 128 * half + 128],
        )
        put_half(outs, places[3], half, jnp.concatenate(pieces, axis=0))


def turn_kernel(places, *refs):
    for number in range(3):
        mine, theirs, out = refs[2 * number], refs[2 * number + 1], refs[8 + number]
        rows = mine.shape[0]
        out[:, :rows] = mine[...].T
        out[:, rows:] = theirs[...].T
    refs[11][...] = add_low(refs[6][...], refs[7][...])


def late_kernel(
    keeping,
    places,
    hidden_cols,
    grad_pre,
    grad_pre_other,
    active_cols,
    grad_low,
    grad_low_other,
    attend_cols,
    attend_rows,
    attend_rows_other,
    position,
    *outs,
):
    step = pl.program_id(0)
    half = places[3] if keeping else 1 - places[3]

    def blocks(left, mine, theirs):
        return low(matmul(left[...], jnp.concatenate([mine[...], theirs[...]], axis=0)))

    @pl.when(step == 0)
    def _():
        outs[0][...] = blocks(hidden_cols, grad_pre, grad_pre_other)

    @pl.when(step == 1)
    def _():
        outs[1][...] = blocks(active_cols, grad_low, grad_low_other)

    @pl.when((step == 2) & (places[0] + half < 2))
    def _():
        outs[2][...] = blocks(attend_cols, attend_rows, attend_rows_other)

    @pl.when((step == 2) & (places[0] + half == 2))
    def _():
        outs[2][...] = position[...]


def late_blocks(keeping, places, cols, grad_pre, pair):
    hidden_cols, active_cols, attend_cols, position = cols
    rows = pair[0].shape[0]

    def half(p, stripe):
        return p[stripe] if keeping else 1 - p[stripe]

    def whole(shape):
        return pl.BlockSpec(shape, lambda i, p: (0, 0))

    def attend_column(i, p):
        return (0, jnp.where(p[0] == 0, 2 + half(p, 3), 4))

    block = (rows, 512)
    return list(
        pl.pallas_call(
            functools.partial(late_kernel, keeping),
            grid_spec=pltpu.PrefetchScalarGridSpec(
                num_scalar_prefetch=1,
                grid=(3,),
                in_specs=[
                    whole(hidden_cols.shape),
                    pl.BlockSpec(block, lambda i, p: (0, half(p, 1))),
                    pl.BlockSpec(block, lambda i, p: (0, half(p, 1))),
                    pl.BlockSpec((512, 2 * rows), lambda i, p: (half(p, 2), 0)),
                    pl.BlockSpec(block, lambda i, p: (0, 5)),
                    pl.BlockSpec(block, lambda i, p: (0, 5)),
                    whole(attend_cols.shape),
                    pl.BlockSpec(block, attend_column),
                    pl.BlockSpec(block, attend_column),
                    whole(position.shape),
                ],
                out_specs=[whole((512, 512))] * 3,
            ),
            out_shape=[jax.ShapeDtypeStruct((512, 512), jnp.bfloat16)] * 3,
            compiler_params=pltpu.CompilerParams(vmem_limit_bytes=SUM_LIMIT if keeping else VMEM_LIMIT),
            cost_estimate=pl.CostEstimate(
                flops=6 * 512 * 512 * 2 * rows, bytes_accessed=6 * 10**6, transcendentals=0
            ),
        )(
            places,
            hidden_cols,
            grad_pre,
            pair[1],
            active_cols,
            *pair,
            attend_cols,
            *pair,
            position,
        )
    )


def columns(pair, width, number, by_core=False):
    index = (lambda numbers: number + numbers[0]) if by_core else number
    return [Part(array, (array.shape[0], width), (0, index)) for array in pair]


def block_sums(kernel, places, stripes, operands):
    blocks = vmem_call(
        kernel,
        [((512, 512), jnp.bfloat16)] * (2 * stripes),
        (),
        [part for pair in operands for part in pair],
        cost=7 * 10**8 * stripes,
        numbers=(places,),
    )
    return blocks[::2], blocks[1::2]


def spread_kernel(count, places, *refs):
    for source, out in zip(refs[:count], refs[-count:]):
        out[...] = wide(source[...]).reshape(out.shape)


def spread_blocks(core, halves, stripes, shapes, bases):
    def source(height, start):
        return pl.BlockSpec((height, 512), lambda i, places: (start // height + i, 0))

    def quarter(p, stripe):
        return 2 * p[0] + p[stripe]

    in_specs = [
        source(512, 0),
        source(512, 0),
        source(128, 0),
        source(64, 256),
        source(64, 384),
        source(256, 512),
    ]
    out_specs = [
        pl.BlockSpec((1, 512, 512), lambda i, p: (1 - i, 0, quarter(p, 1))),
        pl.BlockSpec((1, 512, 512), lambda i, p: (1 - i, quarter(p, 2), 0)),
        pl.BlockSpec((128, 512), lambda i, p: (2 * p[3] + i, p[0])),
        pl.BlockSpec((64, 512), lambda i, p: (2 * quarter(p, 3) + i, 0)),
        pl.BlockSpec((64, 512), lambda i, p: (2 * quarter(p, 3) + i, 0)),
        pl.BlockSpec((1, 256, 512), lambda i, p: (quarter(p, 3), i, 0)),
    ]
    pieces = [stripes[0], stripes[1]] + [stripes[2]] * 4
    return list(
        pl.pallas_call(
            functools.partial(spread_kernel, len(pieces)),
            grid_spec=pltpu.PrefetchScalarGridSpec(
                num_scalar_prefetch=1,
                grid=(2,),
                in_specs=in_specs + [pl.BlockSpec(memory_space=pl.ANY)] * len(bases),
                out_specs=out_specs,
            ),
            out_shape=[jax.ShapeDtypeStruct(shape, jnp.float32) for shape in shapes],
            input_output_aliases={1 + len(pieces) + n: n for n in range(len(bases))},
            compiler_params=pltpu.CompilerParams(vmem_limit_bytes=VMEM_LIMIT),
            cost_estimate=pl.CostEstimate(
                flops=0, bytes_accessed=6 * 512 * 3072, transcendentals=0
            ),
        )(jnp.concatenate([core, halves]), *pieces, *bases)
    )


def angle_tables(frame_count, features):
    halves = jnp.arange(features // 2, dtype=jnp.int32).astype(jnp.float32)
    frequencies = jnp.exp(halves * (-2.0 * math.log(10000.0) / features))
    fine = 32
    low_angles = jnp.arange(fine, dtype=jnp.int32).astype(jnp.float32)[:, None] * frequencies
    high_angles = (fine * jnp.arange(frame_count // fine, dtype=jnp.int32)).astype(jnp.float32)[
        :, None
    ] * frequencies
    low_sin, low_cos = jnp.sin(low_angles)[None], jnp.cos(low_angles)[None]
    high_sin, high_cos = jnp.sin(high_angles)[:, None], jnp.cos(high_angles)[:, None]
    sines = high_sin * low_cos + high_cos * low_sin
    cosines = high_cos * low_cos - high_sin * low_sin
    shape = (frame_count, features // 2)
    return sines.reshape(shape), cosines.reshape(shape)


def heads_out(blocks, groups):
    return lax.all_to_all(jnp.tile(blocks, (groups, 1, 1)), "seq", 0, 0, tiled=True)


def rows_dot(first_operand, second_operand):
    return lax.dot_general(
        first_operand, second_operand, (((1,), (1,)), ((), ())), preferred_element_type=jnp.float32
    )


def lane_side(shape, utterance):
    return (lax.broadcasted_iota(jnp.int32, shape, 1) // HEAD_DIM) == utterance


def turned_queries(content, shift, weight, sines, cosines):
    offset = (content.astype(jnp.float32) + shift).astype(jnp.bfloat16)
    half = sines.shape[1]
    spread = jnp.dot(offset, weight, preferred_element_type=jnp.float32)
    sin_part, cos_part = spread[:, :half], spread[:, half:]
    return (
        offset,
        (sin_part * sines + cos_part * cosines).astype(jnp.bfloat16),
        (cos_part * sines - sin_part * cosines).astype(jnp.bfloat16),
    )


def attend_kernel(
    limits,
    content,
    keys,
    values,
    shift,
    weight,
    sines,
    cosines,
    table,
    weights_out,
    attended_out,
    held,
):
    scale = HEAD_DIM ** (-0.5)
    content_rows = content[...]
    key_side = jnp.concatenate([table[...], keys[...]], axis=1)
    places = lax.broadcasted_iota(jnp.int32, (1, table.shape[0]), 1)
    attended = None
    for utterance in range(limits.shape[0]):
        ours = lane_side(content_rows.shape, utterance)
        mine = jnp.where(ours, content_rows, jnp.zeros_like(content_rows))
        moved = jnp.where(ours, shift[...], 0.0)
        _, turned_cos, turned_sin = turned_queries(
            mine, moved, weight[...], sines[...], cosines[...]
        )
        query_side = jnp.concatenate([turned_cos, turned_sin, mine], axis=1) * scale
        scores = rows_dot(query_side.astype(jnp.bfloat16), key_side)
        scores = jnp.where(places < limits[utterance], scores, -1000000000.0)
        raised = jnp.exp(scores - jnp.max(scores, axis=1, keepdims=True))
        totals = jnp.sum(raised, axis=1, keepdims=True)
        weights = (raised * (1.0 / totals)).astype(jnp.bfloat16)
        weights_out[utterance] = weights
        part = jnp.dot(weights, values[...], preferred_element_type=jnp.float32)
        attended = part if attended is None else jnp.where(ours, part, attended)
    if held is None:
        attended_out[...] = attended.astype(jnp.bfloat16)
        return
    step = pl.program_id(0)
    height = attended.shape[0]
    block = attended_out.shape[1] - 2 * HALO
    held[pl.ds(pl.multiple_of(HALO + step * height, 8), height), :] = attended
    for number in range(height // block):
        attended_out[step * (height // block) + number, 0:block, :] = attended[
            number * block : (number + 1) * block
        ].astype(jnp.bfloat16)

    @pl.when(step == pl.num_programs(0) - 1)
    def _():
        edge = jnp.zeros((HALO, held.shape[1]), jnp.float32)
        held[0:HALO, :] = edge
        held[held.shape[0] - HALO :, :] = edge
        for number in range(attended_out.shape[0]):
            start = number * block
            sides = jnp.concatenate(
                [
                    held[start : start + HALO, :],
                    held[start + HALO + block : start + 2 * HALO + block, :],
                ],
                axis=0,
            )
            attended_out[number, block:, :] = sides.astype(jnp.bfloat16)


def attend_back_kernel(
    weights,
    content,
    grads,
    keys,
    values,
    shift,
    weight,
    sines,
    cosines,
    table,
    *outs,
):
    step = pl.program_id(0)
    query_out, pairs_out, weight_out, sums_out, key_sums, value_sums = (None,) * (
        6 - len(outs)
    ) + outs
    scale = HEAD_DIM ** (-0.5)

    @pl.when(step == 0)
    def _():
        key_sums[...] = jnp.zeros_like(key_sums)
        value_sums[...] = jnp.zeros_like(value_sums)
        weight_out[...] = jnp.zeros_like(weight_out)
        sums_out[...] = jnp.zeros_like(sums_out)

    content_rows, grad_rows = content[...], grads[...]
    content_cols = content_rows.T
    grad_cols = grad_rows.T
    key_side = jnp.concatenate([table[...], keys[...]], axis=1)
    half = sines.shape[1]
    grad_content = grad_position = None
    for utterance in range(weights.shape[0]):
        low, high = utterance * HEAD_DIM, (utterance + 1) * HEAD_DIM
        ours = lane_side(content_rows.shape, utterance)
        probs = weights[utterance]
        wide = probs.astype(jnp.float32)
        grad_mine = jnp.where(ours, grad_rows, jnp.zeros_like(grad_rows)) * scale
        grad_probs = rows_dot(grad_mine.astype(jnp.bfloat16), values[...])
        product = wide * grad_probs
        inner = jnp.sum(product, axis=1, keepdims=True)
        grad_scores = (product - wide * inner).astype(jnp.bfloat16)
        value_sums[low:high, :] += jnp.dot(
            grad_cols[low:high, :], probs, preferred_element_type=jnp.float32
        )
        key_sums[low:high, :] += jnp.dot(
            content_cols[low:high, :], grad_scores, preferred_element_type=jnp.float32
        )
        grad_side = jnp.dot(grad_scores, key_side, preferred_element_type=jnp.float32)
        grad_cos_table = grad_side[:, :half]
        grad_sin_table = grad_side[:, half : 2 * half]
        from_table = jnp.concatenate(
            [
                grad_cos_table * sines[...] - grad_sin_table * cosines[...],
                grad_cos_table * cosines[...] + grad_sin_table * sines[...],
            ],
            axis=1,
        ).astype(jnp.bfloat16)
        offset = (content_rows.astype(jnp.float32) + shift[...]).astype(jnp.bfloat16)
        weight_out[...] += jnp.dot(
            offset.T[low:high, :], from_table, preferred_element_type=jnp.float32
        )
        content_part = grad_side[:, 2 * half :]
        position_part = rows_dot(from_table, weight[...])
        if grad_content is None:
            grad_content, grad_position = content_part, position_part
        else:
            grad_content = jnp.where(ours, content_part, grad_content)
            grad_position = jnp.where(ours, position_part, grad_position)
    grad_query = (grad_content + grad_position).astype(jnp.bfloat16)
    height, lanes = grad_query.shape
    if query_out is None:
        pairs_out[pl.ds(pl.multiple_of(step * height, 16), height), 0:lanes] = grad_query
    else:
        query_out[...] = grad_query
    sums_out[0:1, :] += jnp.sum(grad_content, axis=0, keepdims=True)
    sums_out[1:2, :] += jnp.sum(grad_position, axis=0, keepdims=True)

    @pl.when(step == pl.num_programs(0) - 1)
    def _():
        first = pairs_out.shape[1] - 2 * lanes
        pairs_out[:, first : first + lanes] = key_sums[...].T.astype(jnp.bfloat16)
        pairs_out[:, first + lanes :] = value_sums[...].T.astype(jnp.bfloat16)


def query_block(frames_all):
    return 256 if frames_all <= 1024 else 128


def whole_block(shape):
    return pl.BlockSpec(shape, lambda i: (0,) * len(shape))


def row_block(height, width):
    return pl.BlockSpec((height, width), lambda i: (i, 0))


def attend_heads(limits, content, arrived, shift, weight, sines, cosines, table, block):
    utterances = limits.shape[0]
    query_frames, lanes = content.shape[0], arrived.shape[1] // 3
    frames_all, table_width = table.shape
    height = query_block(frames_all)
    chunked = query_frames == frames_all and height % block == 0
    chunks = (frames_all // block, block + 2 * HALO, lanes)
    kernel = attend_kernel
    if not chunked:
        kernel = functools.partial(attend_kernel, held=None)
    return pl.pallas_call(
        kernel,
        grid=(query_frames // height,),
        in_specs=[
            pl.BlockSpec(memory_space=pltpu.SMEM),
            row_block(height, lanes),
            pl.BlockSpec((frames_all, lanes), lambda i: (0, 1)),
            pl.BlockSpec((frames_all, lanes), lambda i: (0, 2)),
            whole_block(shift.shape),
            whole_block(weight.shape),
            row_block(height, sines.shape[1]),
            row_block(height, sines.shape[1]),
            whole_block(table.shape),
        ],
        out_specs=[
            pl.BlockSpec((utterances, height, frames_all), lambda i: (0, i, 0)),
            whole_block(chunks) if chunked else row_block(height, lanes),
        ],
        out_shape=[
            jax.ShapeDtypeStruct((utterances, query_frames, frames_all), jnp.bfloat16),
            jax.ShapeDtypeStruct(chunks if chunked else (query_frames, lanes), jnp.bfloat16),
        ],
        scratch_shapes=[pltpu.VMEM((frames_all + 2 * HALO, lanes), jnp.float32)] * chunked,
        compiler_params=pltpu.CompilerParams(vmem_limit_bytes=VMEM_LIMIT),
        cost_estimate=pl.CostEstimate(
            flops=2 * utterances * query_frames * frames_all * (table_width + 256),
            bytes_accessed=2 * utterances * query_frames * frames_all,
            transcendentals=utterances * query_frames * frames_all,
        ),
    )(limits, content, arrived, arrived, shift, weight, sines, cosines, table)


def attend_heads_back(
    weights, content, grads, arrived, shift, weight, sines, cosines, table
):
    utterances, query_frames, frames_all = weights.shape
    lanes = arrived.shape[1] // 3
    height = query_block(frames_all)
    joined = query_frames == frames_all
    width = (3 if joined else 2) * lanes
    return pl.pallas_call(
        attend_back_kernel,
        grid=(query_frames // height,),
        in_specs=[
            pl.BlockSpec((utterances, height, frames_all), lambda i: (0, i, 0)),
            row_block(height, lanes),
            row_block(height, lanes),
            pl.BlockSpec((frames_all, lanes), lambda i: (0, 1)),
            pl.BlockSpec((frames_all, lanes), lambda i: (0, 2)),
            whole_block(shift.shape),
            whole_block(weight.shape),
            row_block(height, sines.shape[1]),
            row_block(height, sines.shape[1]),
            whole_block(table.shape),
        ],
        out_specs=([] if joined else [row_block(height, lanes)])
        + [
            whole_block((frames_all, width)),
            whole_block((HEAD_DIM, table.shape[1])),
            whole_block((8, lanes)),
        ],
        out_shape=(
            [] if joined else [jax.ShapeDtypeStruct((query_frames, lanes), jnp.bfloat16)]
        )
        + [
            jax.ShapeDtypeStruct((frames_all, width), jnp.bfloat16),
            jax.ShapeDtypeStruct((HEAD_DIM, table.shape[1]), jnp.float32),
            jax.ShapeDtypeStruct((8, lanes), jnp.float32),
        ],
        scratch_shapes=[
            pltpu.VMEM((lanes, frames_all), jnp.float32),
            pltpu.VMEM((lanes, frames_all), jnp.float32),
        ],
        compiler_params=pltpu.CompilerParams(vmem_limit_bytes=VMEM_LIMIT),
        cost_estimate=pl.CostEstimate(
            flops=2 * utterances * query_frames * frames_all * (table.shape[1] + 512),
            bytes_accessed=2 * utterances * query_frames * frames_all,
            transcendentals=0,
        ),
    )(weights, content, grads, arrived, arrived, shift, weight, sines, cosines, table)


def shards(
    frames,
    lengths,
    out_grad,
    norm_gain,
    norm_bias,
    feed_in,
    feed_in_bias,
    feed_out,
    feed_out_bias,
    attend_in,
    attend_vectors,
    attend_out,
    mixer_in,
    mixer_in_bias,
    depthwise,
    mixer_vectors,
    mixer_out,
    batch_gain,
    batch_shift,
    running_mean,
    running_variance,
):
    utt_rows, block_frames, features = frames.shape
    rows = utt_rows * block_frames
    seq_count = lax.axis_size("seq")
    seq_index = lax.axis_index("seq")
    count = lax.axis_size("utt") * seq_count
    frames_all = block_frames * seq_count
    groups = seq_count // HEADS
    head, group = seq_index % HEADS, seq_index // HEADS
    query_frames = frames_all // groups
    lanes = utt_rows * HEAD_DIM
    info = jnp.concatenate(
        [(seq_index * block_frames).reshape(1), lengths, jnp.full((1,), frames_all, jnp.int32)]
    )
    hidden_units = feed_in.shape[2]
    f32, bf16 = jnp.float32, jnp.bfloat16
    flat_frames = frames.reshape(rows, features)
    square, broad = (rows, features), (rows, hidden_units)
    extended = (utt_rows * (block_frames + 2 * HALO), features)
    row_flops = 2 * rows * features
    bind = functools.partial
    edge = ((utt_rows, 2 * HALO, features), f32)
    feed_scratch = [
        pltpu.VMEM((features, hidden_units), bf16),
        pltpu.VMEM((hidden_units, features), bf16),
    ]
    attend_scratch = pltpu.VMEM((3, features, features), bf16)
    (
        edge_head,
        edge_tail,
        after_first,
        slope_first,
        entry_pack,
        sent,
    ) = vmem_call(
        bind(entry_kernel, utt_rows),
        [
            edge,
            edge,
            (square, f32),
            (broad, bf16),
            ((rows, hidden_units + 2 * features), bf16),
            ((HEADS, block_frames, 3 * lanes), bf16),
        ],
        (),
        (
            flat_frames,
            norm_gain,
            norm_bias,
            feed_in_bias,
            feed_out_bias,
            attend_vectors,
            Part(out_grad, (utt_rows, HALO, features), (0, 0, 0)),
            Part(out_grad, (utt_rows, HALO, features), (0, block_frames // HALO - 1, 0)),
        ),
        scratch=feed_scratch + [attend_scratch, pltpu.SemaphoreType.DMA((3,))],
        cost=row_flops * (2 * hidden_units + 3 * features),
        held=(feed_in, feed_out, attend_in),
    )
    sent, edge_head, edge_tail = tie(sent, edge_head, edge_tail)
    before, behind = from_neighbours(edge_head, edge_tail)
    after_sides, grad_sides = vmem_call(
        sides_kernel,
        [((2 * utt_rows * HALO, features), f32)] * 2,
        (),
        (before, behind, norm_gain, norm_bias, feed_in_bias, feed_out_bias),
        scratch=feed_scratch + [pltpu.SemaphoreType.DMA((2,))],
        cost=row_flops * 2 * hidden_units // 4,
        held=(feed_in, feed_out),
    )
    arrived, after_sides, grad_sides = tie(heads_out(sent, groups), after_sides, grad_sides)
    arrived = arrived.reshape(frames_all, 3 * lanes)
    start_query = group * query_frames
    head_content = arrived
    if groups > 1:
        head_content = lax.dynamic_slice_in_dim(arrived, start_query, query_frames, 0)
    head_vectors = lax.dynamic_slice_in_dim(
        attend_vectors.astype(f32), head * HEAD_DIM, HEAD_DIM, 1
    )
    head_shift = jnp.tile((head_vectors[4] - head_vectors[3])[None], (1, utt_rows))
    head_weight = lax.dynamic_slice_in_dim(attend_in[3], head * HEAD_DIM, HEAD_DIM, 1).reshape(
        features // 2, 2, HEAD_DIM
    )
    head_weight = jnp.tile(
        jnp.transpose(head_weight, (2, 1, 0)).reshape(HEAD_DIM, features), (utt_rows, 1)
    )
    sines, cosines = angle_tables(frames_all, features)
    key_table = jnp.concatenate([cosines, sines], axis=1).astype(bf16)
    query_sin = lax.dynamic_slice_in_dim(sines, start_query, query_frames, 0)
    query_cos = lax.dynamic_slice_in_dim(cosines, start_query, query_frames, 0)
    weights, head_attended = attend_heads(
        lengths,
        head_content,
        arrived,
        head_shift,
        head_weight,
        query_sin,
        query_cos,
        key_table,
        block_frames,
    )

    def frames_back(blocks):
        width = blocks.shape[-1]
        blocks = blocks.reshape(1, HEADS, block_frames, width)
        if groups > 1:
            blocks = lax.dynamic_update_slice_in_dim(
                jnp.zeros((groups,) + blocks.shape[1:], blocks.dtype), blocks, group, 0
            )
        blocks = lax.all_to_all(
            blocks.reshape(seq_count, block_frames, width), "seq", 0, 0, tiled=True
        ).reshape(groups, HEADS, block_frames, width)
        return lax.dynamic_slice_in_dim(blocks, group, 1, 0)[0]

    head_attended, own_limits = tie(head_attended, lengths)
    all_limits = lax.all_gather(own_limits, "utt", tiled=True)
    if head_attended.ndim == 2:
        placed = lax.dynamic_update_slice_in_dim(
            jnp.zeros((frames_all + 2 * HALO, lanes), bf16), head_attended, HALO + start_query, 0
        )
        main, before, behind = (
            placed[start : start + frames_all].reshape(seq_count, block_frames, lanes)
            for start in (HALO, 0, 2 * HALO)
        )
        head_attended = jnp.concatenate([main, before[:, :HALO], behind[:, -HALO:]], axis=1)
    attended_blocks = lax.all_to_all(head_attended, "seq", 0, 0, tiled=True)
    attended_blocks, all_limits = tie(attended_blocks, all_limits)
    if groups > 1:
        attended_blocks = jnp.sum(
            attended_blocks.reshape((groups, HEADS) + attended_blocks.shape[1:]), axis=0
        )
    taps = depthwise.T
    padded = pltpu.VMEM((utt_rows, block_frames + 2 * HALO + 16, features), f32)
    (
        after_attend,
        mixer_pack,
        linear_half,
        gate_half,
        gated,
        convolved,
        shared,
    ) = vmem_call(
        bind(mixer_kernel, utt_rows),
        [
            (extended, f32),
            ((rows, 2 * features), bf16),
            (square, f32),
            (square, f32),
            (extended, bf16),
            (extended, f32),
            ((8 * count, 128), f32),
        ],
        (info,),
        (
            attended_blocks,
            after_first,
            after_sides,
            norm_gain,
            norm_bias,
            attend_out,
            attend_vectors,
            mixer_in,
            mixer_in_bias.reshape(1, -1),
            taps,
            mixer_vectors,
        ),
        scratch=(padded,),
        cost=row_flops * 3 * features,
    )
    (
        layer_output,
        grad_mixer,
        grad_batch,
        normed_batch,
        second_pack,
        shared,
        batch_rows,
        middle_rows,
    ) = vmem_call(
        bind(middle_kernel, utt_rows, seq_count),
        [
            (square, f32),
            (square, f32),
            (extended, f32),
            (extended, f32),
            ((rows, 2 * hidden_units + 4 * features), bf16),
            ((8 * count, 128), f32),
            ((8, features), f32),
            ((16, features), f32),
        ],
        (all_limits,),
        (
            convolved,
            all_shared(shared),
            after_attend,
            out_grad.reshape(rows, features),
            grad_sides,
            norm_gain,
            norm_bias,
            batch_gain.reshape(1, -1),
            batch_shift.reshape(1, -1),
            running_mean.reshape(1, -1),
            running_variance.reshape(1, -1),
            mixer_out,
            mixer_vectors,
            feed_in_bias,
            feed_out_bias,
        ),
        scratch=feed_scratch + [pltpu.SemaphoreType.DMA((2,))],
        cost=row_flops * (4 * hidden_units + 2 * features),
        held=(feed_in, feed_out),
    )
    phases = list(zip(*step_orders()))
    near = axis_bits("utt")[0]
    core = side(near).reshape(1)
    halves = jnp.stack([side(step) for step in phases[0]])
    places = jnp.concatenate([core, halves])
    half_units, half_features = hidden_units // 2, features // 2

    def with_pair(array):
        return [array, swap(array, near)]

    second_pair = with_pair(second_pack)
    second_sent, second_kept = block_sums(
        second_kernel,
        places,
        2,
        [
            columns(second_pair, features, 8),
            columns(second_pair, half_units, 0, True),
            columns(second_pair, half_units, 2, True),
            columns(second_pair, features, 9),
        ],
    )
    second_pair, second_sent, second_kept, shared = tie(
        second_pair, second_sent, second_kept, all_shared(shared)
    )
    (
        batch_grads,
        grad_attend,
        mixer_back_pack,
        grad_blocks,
        mixer_rows,
    ) = vmem_call(
        bind(mixer_back_kernel, utt_rows),
        [
            ((8, features), f32),
            (square, f32),
            ((rows, 3 * features), bf16),
            ((HEADS, block_frames, lanes), bf16),
            ((16, features), f32),
        ],
        (info,),
        (
            grad_batch,
            normed_batch,
            shared,
            batch_rows,
            batch_gain.reshape(1, -1),
            gated,
            linear_half,
            gate_half,
            grad_mixer,
            after_attend,
            norm_gain,
            taps,
            mixer_in,
            attend_out,
        ),
        scratch=(padded, padded),
        cost=row_flops * 4 * features,
    )
    mixer_pair, mixer_back_pair = with_pair(mixer_pack), with_pair(mixer_back_pack)
    third_sent, third_kept = block_sums(
        mixer_blocks_kernel,
        places,
        1,
        [
            columns(mixer_pair, features, 1),
            columns(mixer_back_pair, features, 0, True),
            columns(second_pair, half_features, 20, True),
            columns(second_pair, features, 11),
            columns(mixer_pair, half_features, 0, True),
            columns(mixer_back_pair, features, 2),
        ],
    )
    early_sent, early_kept = second_sent + third_sent, second_kept + third_kept
    early_arrived = swap_all(early_sent, phases[0])
    head_grad = heads_out(grad_blocks, groups).reshape(frames_all, lanes)
    if groups > 1:
        head_grad = lax.dynamic_slice_in_dim(head_grad, start_query, query_frames, 0)
    head_grad, early_kept = tie(head_grad, early_kept)
    *head_grads, head_weight_grad, head_sums = attend_heads_back(
        weights,
        head_content,
        head_grad,
        arrived,
        head_shift,
        head_weight,
        query_sin,
        query_cos,
        key_table,
    )
    head_grads, head_weight_grad, head_sums, early_arrived = tie(
        head_grads, head_weight_grad, head_sums, early_arrived
    )
    grad_blocks = head_grads[-1].reshape(seq_count, block_frames, -1)
    returned = lax.all_to_all(grad_blocks, "seq", 0, 0, tiled=True)
    if groups > 1:
        returned = jnp.sum(
            returned.astype(f32).reshape(groups, HEADS, block_frames, 2 * lanes), axis=0
        ).astype(bf16)
        returned = jnp.concatenate([frames_back(head_grads[0]), returned], axis=2)
    head_weight_grad = jnp.transpose(
        head_weight_grad.reshape(HEAD_DIM, 2, features // 2), (2, 1, 0)
    ).reshape(features, HEAD_DIM)
    position_weight_grad = lax.dynamic_update_slice_in_dim(
        jnp.zeros((features, features), f32), head_weight_grad, head * HEAD_DIM, 1
    )
    head_vector_grads = lax.dynamic_update_slice_in_dim(
        jnp.zeros((8, features), f32),
        jnp.sum(head_sums.reshape(8, utt_rows, HEAD_DIM), axis=1),
        head * HEAD_DIM,
        1,
    )
    def next_phase(kept, arrived_rows, steps):
        sent_rows, kept = fold_rows([(kept, arrived_rows)], steps)
        return kept, swap_all(tie(sent_rows)[0], steps)

    early_kept, early_arrived = next_phase(early_kept, early_arrived, phases[1])
    entry_pair = with_pair(entry_pack)
    position_pair = with_pair(position_weight_grad.astype(bf16))
    entry_cols = vmem_call(
        turn_kernel,
        [
            ((features, 2 * rows), bf16),
            ((half_units, 2 * rows), bf16),
            ((features, 2 * rows), bf16),
            ((features, features), bf16),
        ],
        (),
        columns(entry_pair, features, 4)
        + columns(entry_pair, half_units, 0, True)
        + columns(entry_pair, features, 5)
        + position_pair,
        numbers=(places,),
    )
    returned, early_arrived, entry_cols = tie(returned, early_arrived, entry_cols)
    (
        frames_grad,
        entry_back_pack,
        grad_pre_first,
        entry_rows,
    ) = vmem_call(
        entry_back_kernel,
        [
            (square, f32),
            ((rows, half_units + 4 * features), bf16),
            ((rows, half_units), bf16),
            ((16, features), f32),
        ],
        (core,),
        (
            returned,
            grad_attend,
            flat_frames,
            after_first,
            slope_first,
            norm_gain,
        ),
        scratch=feed_scratch + [attend_scratch, pltpu.SemaphoreType.DMA((3,))],
        cost=row_flops * (2 * hidden_units + 3 * features),
        held=(feed_in, feed_out, attend_in),
    )
    late_factors = (entry_cols, grad_pre_first, with_pair(entry_back_pack))
    late_sent = late_blocks(False, places, *late_factors)
    late_sent, late_factors, middle_rows = tie(late_sent, late_factors, middle_rows)
    late_arrived = swap_all(late_sent, phases[0])
    late_kept = late_blocks(True, places, *late_factors)
    flat = jnp.concatenate([middle_rows, mixer_rows, entry_rows, head_vector_grads], axis=0)
    flat_steps = [near] + [steps[0] for steps in phases]
    late_arrived, flat = tie(late_arrived, flat)
    for steps in phases[1:]:
        pairs = [(late_kept, late_arrived)]
        if steps is phases[2]:
            pairs = [(early_kept, early_arrived)] + pairs
        parts = 1 if steps in phases[1:3] else 2
        sent_rows, late_kept = fold_rows(pairs, steps, parts)
        (sent_rows,) = tie(sent_rows)
        late_arrived, flat_arrived = tie(swap_all(sent_rows, steps), swap(flat, flat_steps.pop()))
        flat = flat + flat_arrived
    sums = add_rows(late_kept, late_arrived)
    for steps in phases[:0:-1]:
        (sums,) = tie(sums)
        flat_arrived = swap(flat, flat_steps.pop()) if flat_steps else jnp.zeros_like(flat)
        arrived_rows, flat_arrived = tie(swap_all(sums, steps), flat_arrived)
        flat = flat + flat_arrived
        sums = join_rows(sums, arrived_rows, steps)
    (sums,) = tie(sums)
    vector_grads = vmem_call(
        vectors_kernel,
        [
            (norm_gain.shape, f32),
            (norm_bias.shape, f32),
            (feed_in_bias.shape, f32),
            (feed_out_bias.shape, f32),
            (attend_vectors.shape, f32),
            ((1, 2 * features), f32),
            (mixer_vectors.shape, f32),
            ((KERNEL, features), f32),
        ],
        (),
        (flat,),
    )
    vector_grads = list(vector_grads)
    vector_grads[5] = vector_grads[5].reshape(-1)
    vector_grads[7] = vector_grads[7].T
    vector_grads = [*vector_grads, batch_grads[1], batch_grads[0], batch_rows[2], batch_rows[3]]
    arrived_rows = swap_all(sums, phases[0])
    across_rows = swap_all(sums, [near] * 3)
    shapes = [feed_in.shape, feed_out.shape, mixer_in.shape, mixer_out.shape]
    shapes += [attend_out.shape, attend_in.shape]
    spread = spread_blocks(core, halves, sums, shapes, [])
    spread = spread_blocks(1 - core, halves, across_rows, shapes, spread)
    spread, arrived_rows, vector_grads = tie(spread, arrived_rows, vector_grads)
    across_rows = swap_all(arrived_rows, [near] * 3)
    spread = spread_blocks(core, 1 - halves, arrived_rows, shapes, spread)
    (
        feed_in_grad,
        feed_out_grad,
        mixer_in_grad,
        mixer_out_grad,
        attend_out_grad,
        attend_in_grad,
    ) = spread_blocks(1 - core, 1 - halves, across_rows, shapes, spread)
    (
        norm_gain_grad,
        norm_bias_grad,
        feed_in_bias_grad,
        feed_out_bias_grad,
        attend_vectors_grad,
        mixer_in_bias_grad,
        mixer_vectors_grad,
        taps_grad,
        batch_gain_grad,
        batch_shift_grad,
        new_mean,
        new_variance,
    ) = vector_grads
    return (
        layer_output.reshape(frames.shape),
        frames_grad.reshape(frames.shape),
        norm_gain_grad,
        norm_bias_grad,
        feed_in_grad,
        feed_in_bias_grad,
        feed_out_grad,
        feed_out_bias_grad,
        attend_in_grad,
        attend_vectors_grad,
        attend_out_grad,
        mixer_in_grad,
        mixer_in_bias_grad,
        taps_grad,
        mixer_vectors_grad,
        mixer_out_grad,
        batch_gain_grad,
        batch_shift_grad,
        new_mean,
        new_variance,
    )


def solution(mesh):
    return jax.shard_map(
        shards,
        mesh=mesh,
        in_specs=(
            P("utt", "seq", None),
            P("utt"),
            P("utt", "seq", None),
            P(),
            P(),
            P(),
            P(),
            P(),
            P(),
            P(),
            P(),
            P(),
            P(),
            P(),
            P(),
            P(),
            P(),
            P(),
            P(),
            P(),
            P(),
        ),
        out_specs=(
            P("utt", "seq", None),
            P("utt", "seq", None),
            P(),
            P(),
            P(),
            P(),
            P(),
            P(),
            P(),
            P(),
            P(),
            P(),
            P(),
            P(),
            P(),
            P(),
            P(),
            P(),
            P(),
            P(),
        ),
        check_vma=False,
    )
```

profile of v0, /device:TPU:0, one launch (start us, length us, event | category | flops | bytes accessed | tf_op | source)
XLA Modules:
  0.0 325.4 jit_solution(14928623547651915747)
XLA Ops:
  0.7 7.1 %shard_map.356 = (f32[2,16,512]{2,1,0:T(8,128)}, f32[2,16,512]{2,1,0:T(8,128)}, f32[256,512]{1,0:T(8,128)}, bf16[256,2048]{1,0:T(8,128)(2,1)}, bf16[256,3072]{1,0:T(8,128)(2,1)}, /*index=5*/bf16[8,128,384]{2,1,0:T(8,128)(2,1)}) custom-call(f32[256,512]{1,0:T(8,128)} %bitcast.47, bf16[5,512]{1,0:T(8,128)(2,1)} %gains.11, bf16[5,512]{1,0:T(8,128)(2,1)} %biases.7, ...), custom_call_target="tpu_custom_call" | custom-call | flops 1476395008 | bytes 4921316 | tf_op jit(solution)/shard_map/pallas_call | solution.py:144
  7.7 7.3 %all-to-all-start = ((bf16[8,128,384]{2,1,0:T(8,128)(2,1)}), bf16[8,128,384]{2,1,0:T(8,128)(2,1)S(1)}, u32[]{:S(2)}, u32[]{:S(2)}) async-start(bf16[8,128,384]{2,1,0:T(8,128)(2,1)} %get-tuple-element.251), calls=%async_computation | async-start | bytes 1572864 | tf_op jit(solution)/shard_map/all_to_all | solution.py:1131
  15.0 3.9 %collective-permute-start = (f32[2,16,512]{2,1,0:T(8,128)}, f32[2,16,512]{2,1,0:T(8,128)S(1)}, u32[]{:S(2)}, u32[]{:S(2)}) collective-permute-start(f32[2,16,512]{2,1,0:T(8,128)} %get-tuple-element.252), channel_id=1, source_target_pairs={{0,1},{1,2},{2,3},{3,4},{4,5},{5,6},{6,7},{8,9},{9,10},{10,11},{11... | collective-permute-start | bytes 196616 | tf_op jit(solution)/shard_map/ppermute | solution.py:896
  26.8 4.2 %shard_map.357 = (f32[32,512]{1,0:T(8,128)}, f32[32,512]{1,0:T(8,128)}) custom-call(f32[2,16,512]{2,1,0:T(8,128)} %copy-done.26, f32[2,16,512]{2,1,0:T(8,128)} %copy-done.27, bf16[5,512]{1,0:T(8,128)(2,1)} %gains.11, bf16[5,512]{1,0:T(8,128)(2,1)} %biases.7, bf16[2,2048]{1,0:T(2,128)(2,1)} %bias_in.5, bf16[2,512]{1,0:T(2,128)(2,1)} %bias_out.5, ...), custom_call_target="tpu_custom_call" | custom-call | flops 268435456 | bytes 894784 | tf_op jit(solution)/shard_map/pallas_call | solution.py:144
  31.0 4.9 %all-to-all-done = bf16[8,128,384]{2,1,0:T(8,128)(2,1)S(1)} async-done(((bf16[8,128,384]{2,1,0:T(8,128)(2,1)}), bf16[8,128,384]{2,1,0:T(8,128)(2,1)S(1)}, u32[]{:S(2)}, u32[]{:S(2)}) %all-to-all-start) | async-done | bytes 786464 | tf_op jit(solution)/shard_map/all_to_all | solution.py:1131
  36.8 11.8 %shard_map.358 = (bf16[2,1024,1024]{2,1,0:T(8,128)(2,1)}, bf16[8,144,128]{2,1,0:T(8,128)(2,1)}) custom-call(s32[2]{0:T(128)} %limits.1, bf16[1024,384]{1,0:T(8,128)(2,1)} %bitcast.49, bf16[1024,384]{1,0:T(8,128)(2,1)} %bitcast.50, bf16[1024,384]{1,0:T(8,128)(2,1)} %bitcast.51, f32[1,128]{1,0:T(1,128)} %tile.19.shift, bf16[128,512]{1,0:T(8,128)(2,1)} %bitcast.62, ...), custom_call_target="tpu_custom_call" | custom-call | flops 3221225472 | bytes 4194304 | tf_op jit(solution)/shard_map/pallas_call | solution.py:1327
  48.7 8.9 %all-to-all-start.1 = ((bf16[8,144,128]{2,1,0:T(8,128)(2,1)}), bf16[8,144,128]{2,1,0:T(8,128)(2,1)S(1)}, u32[]{:S(2)}, u32[]{:S(2)}) async-start(bf16[8,144,128]{2,1,0:T(8,128)(2,1)} %get-tuple-element.258), calls=%async_computation.1 | async-start | bytes 589824 | tf_op jit(solution)/shard_map/all_to_all | solution.py:1556
  60.2 5.4 %all-reduce.limits = s32[8]{0:T(128)} all-reduce(s32[8]{0:T(128)S(1)} %dynamic-update-slice), channel_id=1, replica_groups=mesh['utt'=4,'seq'=8] {'utt'}, use_global_device_ids=true, to_apply=%add | all-reduce | flops 8 | bytes 64 | tf_op jit(solution)/shard_map/optimization_barrier | solution.py:877
  68.0 4.7 %shard_map.359 = (f32[288,512]{1,0:T(8,128)}, bf16[256,1024]{1,0:T(8,128)(2,1)}, f32[256,512]{1,0:T(8,128)}, f32[256,512]{1,0:T(8,128)}, bf16[288,512]{1,0:T(8,1...) custom-call(s32[4]{0:T(128)} %pad_add_fusion.info, bf16[8,144,128]{2,1,0:T(8,128)(2,1)} %copy-done.22, ...), custom_call_target="tpu_custom_call" | custom-call | flops 402653184 | bytes 1342177 | tf_op jit(solution)/shard_map/pallas_call | solution.py:144
  72.8 3.9 %all-to-all-start.2 = ((f32[32,8,128]{2,1,0:T(8,128)}), f32[32,8,128]{2,1,0:T(8,128)S(1)}, u32[]{:S(2)}, u32[]{:S(2)}) async-start(f32[32,8,128]{2,1,0:T(8,128)} %bitcast.65), calls=%async_computation.2 | async-start | bytes 262144 | tf_op jit(solution)/shard_map/all_to_all | solution.py:891
  77.8 6.4 %all-to-all-done.2 = f32[32,8,128]{2,1,0:T(8,128)S(1)} async-done(((f32[32,8,128]{2,1,0:T(8,128)}), f32[32,8,128]{2,1,0:T(8,128)S(1)}, u32[]{:S(2)}, u32[]{:S(2)}) %all-to-all-start.2) | async-done | bytes 131104 | tf_op jit(solution)/shard_map/all_to_all | solution.py:891
  84.8 9.6 %shard_map.360 = (f32[256,512]{1,0:T(8,128)}, f32[256,512]{1,0:T(8,128)}, f32[288,512]{1,0:T(8,128)}, f32[288,512]{1,0:T(8,128)}, bf16[256,6144]{1,0:T(8,128)(2,...) custom-call(s32[8]{0:T(128)} %all-reduce.limits, f32[288,512]{1,0:T(8,128)} %get-tuple-element.264.convolved, ...), custom_call_target="tpu_custom_call" | custom-call | flops 2415919104 | bytes 8053063 | tf_op jit(solution)/shard_map/pallas_call | solution.py:144
  94.6 2.6 all-to-all-start.3
  97.9 2.7 collective-permute-done.2.refs_1_.refs_3_.refs_5_.refs_7_
  100.5 5.9 %shard_map.361 = (bf16[512,512]{1,0:T(8,128)(2,1)}, bf16[512,512]{1,0:T(8,128)(2,1)}, bf16[512,512]{1,0:T(8,128)(2,1)}, bf16[512,512]{1,0:T(8,128)(2,1)}) custom-call(s32[4]{0:T(128)} %add_add_fusion.1.places, bf16[256,6144]{1,0:T(8,128)(2,1)} %get-tuple-element.289.refs_0_.refs_2_.refs_4_.refs_6_, ...), custom_call_target="tpu_custom_call" | custom-call | flops 1400000000 | bytes 4666666 | tf_op jit(solution)/shard_map/pallas_call | solution.py:144
  107.1 5.9 %shard_map.362 = (f32[8,512]{1,0:T(8,128)}, f32[256,512]{1,0:T(8,128)}, bf16[256,1536]{1,0:T(8,128)(2,1)}, bf16[8,128,128]{2,1,0:T(8,128)(2,1)}, f32[16,512]{1,0:T(8,128)}) custom-call(s32[4]{0:T(128)} %pad_add_fusion.info, f32[288,512]{1,0:T(8,128)} %get-tuple-element.270.grad_batch, f32[288,512]{1,0:T(8,128)} %get-tuple-element.271.normed_batch, ...), custom_call_target="tpu_custom_call" | custom-call | flops 536870912 | bytes 1789569 | tf_op jit(solution)/shard_map/pallas_call | solution.py:144
  113.5 4.0 %all-to-all-start.4 = ((bf16[8,128,128]{2,1,0:T(8,128)(2,1)}), bf16[8,128,128]{2,1,0:T(8,128)(2,1)}, u32[]{:S(2)}, u32[]{:S(2)}) async-start(bf16[8,128,128]{2,1,0:T(8,128)(2,1)} %get-tuple-element.284), calls=%async_computation.4 | async-start | bytes 524288 | tf_op jit(solution)/shard_map/all_to_all | solution.py:1131
  121.5 4.4 %shard_map.363 = (bf16[512,512]{1,0:T(8,128)(2,1)}, bf16[512,512]{1,0:T(8,128)(2,1)}) custom-call(s32[4]{0:T(128)} %add_add_fusion.1.places, bf16[256,1024]{1,0:T(8,128)(2,1)} %get-tuple-element.287.refs_0_.refs_8_, bf16[256,1024]{1,0:T(8,128)(2,1)} %collective-permute-done.3.refs_1_.refs_9_, bf16[256,1536]{1,0:T(8,128)(2,1)} %get-tuple-element.288.refs_2_.refs_10_, ...), custom_call_target="tpu_custom_call" | custom-call | flops 700000000 | bytes 2333333 | tf_op jit(solution)/shard_map/pallas_call | solution.py:144
  127.3 12.9 %shard_map.364 = (bf16[1024,384]{1,0:T(8,128)(2,1)}, f32[64,512]{1,0:T(8,128)}, f32[8,128]{1,0:T(8,128)}) custom-call(bf16[2,1024,1024]{2,1,0:T(8,128)(2,1)} %get-tuple-element.269.weights, bf16[1024,384]{1,0:T(8,128)(2,1)} %bitcast.52, bf16[1024,128]{1,0:T(8,128)(2,1)} %bitcast.23.grads, bf16[1024,384]{1,0:T(8,128)(2,1)} %bitcast.53, ...), custom_call_target="tpu_custom_call" | custom-call | flops 4294967296 | bytes 4194304 | tf_op jit(solution)/shard_map/pallas_call | solution.py:1367
  140.3 4.2 %all-to-all-start.5 = ((bf16[8,128,384]{2,1,0:T(8,128)(2,1)}), bf16[8,128,384]{2,1,0:T(8,128)(2,1)}, u32[]{:S(2)}, u32[]{:S(2)}) async-start(bf16[8,128,384]{2,1,0:T(8,128)(2,1)} %bitcast.55), calls=%async_computation.5 | async-start | bytes 1572864 | tf_op jit(solution)/shard_map/all_to_all | solution.py:1738
  148.8 3.0 shard_map.365
  157.7 4.3 %shard_map.366 = (bf16[512,512]{1,0:T(8,128)(2,1)}, bf16[1024,512]{1,0:T(8,128)(2,1)}, bf16[512,512]{1,0:T(8,128)(2,1)}, bf16[512,512]{1,0:T(8,128)(2,1)}) custom-call(s32[4]{0:T(128)} %add_add_fusion.1.places, bf16[256,3072]{1,0:T(8,128)(2,1)} %get-tuple-element.312.refs_0_.refs_2_.refs_4_, ...), custom_call_target="tpu_custom_call" | custom-call | tf_op jit(solution)/shard_map/pallas_call | solution.py:144
  162.0 4.9 %collective-permute-done.9.refs_5_ = bf16[256,512]{1,0:T(8,128)(2,1)S(1)} collective-permute-done((bf16[256,512]{1,0:T(8,128)(2,1)}, bf16[256,512]{1,0:T(8,128)(2,1)S(1)}, u32[]{:S(2)}, u32[]{:S(2)}) %collective-permute-start.9) | collective-permute-done | bytes 262176 | tf_op jit(solution)/shard_map/ppermute | solution.py:729
  166.9 7.4 %shard_map.367 = (f32[256,512]{1,0:T(8,128)}, bf16[256,3072]{1,0:T(8,128)(2,1)}, bf16[256,1024]{1,0:T(8,128)(2,1)}, f32[16,512]{1,0:T(8,128)}) custom-call(s32[1]{0:T(128)} %bitcast.17.core, bf16[8,128,384]{2,1,0:T(8,128)(2,1)} %all-to-all-done.5.returned, f32[256,512]{1,0:T(8,128)} %get-tuple-element.319.grad_attend, f32[256,512]{1,0:T(8,128)} %bitcast.48, ...), custom_call_target="tpu_custom_call" | custom-call | flops 1476395008 | bytes 4921316 | tf_op jit(solution)/shard_map/pallas_call | solution.py:144
  174.4 3.7 %collective-permute-done.13.grad_pre_other.grad_low_other.attend_rows_other = bf16[256,3072]{1,0:T(8,128)(2,1)} collective-permute-done((bf16[256,3072]{1,0:T(8,128)(2,1)}, bf16[256,3072]{1,0:T(8,128)(2,1)}, u32[]{:S(2)}, u32[]{:S(2)}) %collective-permute-start.13) | collective-permute-done | bytes 1572896 | tf_op jit(solution)/shard_map/ppermute | solution.py:729
  178.2 5.5 %shard_map.368 = (bf16[512,512]{1,0:T(8,128)(2,1)}, bf16[512,512]{1,0:T(8,128)(2,1)}, bf16[512,512]{1,0:T(8,128)(2,1)}) custom-call(s32[4]{0:T(128)} %add_add_fusion.1.places, bf16[512,512]{1,0:T(8,128)(2,1)} %get-tuple-element.334.hidden_cols, bf16[256,1024]{1,0:T(8,128)(2,1)} %get-tuple-element.335.grad_pre, ...), custom_call_target="tpu_custom_call" | custom-call | flops 805306368 | bytes 6000000 | tf_op jit(solution)/shard_map/pallas_call | solution.py:1011
  192.9 3.2 shard_map.369
  202.9 3.2 collective-permute-start.20
  206.1 3.4 %collective-permute-done.20 = f32[56,512]{1,0:T(8,128)S(1)} collective-permute-done((f32[56,512]{1,0:T(8,128)S(1)}, f32[56,512]{1,0:T(8,128)S(1)}, u32[]{:S(2)}, u32[]{:S(2)}) %collective-permute-start.20) | collective-permute-done | bytes 114720 | tf_op jit(solution)/shard_map/ppermute | solution.py:729
  217.3 8.3 %collective-permute-done.24 = f32[56,512]{1,0:T(8,128)S(1)} collective-permute-done((f32[56,512]{1,0:T(8,128)S(1)}, f32[56,512]{1,0:T(8,128)S(1)}, u32[]{:S(2)}, u32[]{:S(2)}) %collective-permute-start.24) | collective-permute-done | bytes 114720 | tf_op jit(solution)/shard_map/ppermute | solution.py:729
  226.3 2.4 collective-permute-start.25
  228.7 2.4 collective-permute-start.26
  232.6 3.7 %collective-permute-done.28 = f32[56,512]{1,0:T(8,128)S(1)} collective-permute-done((f32[56,512]{1,0:T(8,128)S(1)}, f32[56,512]{1,0:T(8,128)S(1)}, u32[]{:S(2)}, u32[]{:S(2)}) %collective-permute-start.28) | collective-permute-done | bytes 114720 | tf_op jit(solution)/shard_map/ppermute | solution.py:729
  236.4 2.9 collective-permute-done.27.refs_5_
  239.4 2.7 collective-permute-start.30
  242.2 2.8 collective-permute-start.31
  245.1 4.8 %collective-permute-done.32 = f32[56,512]{1,0:T(8,128)S(1)} collective-permute-done((f32[56,512]{1,0:T(8,128)S(1)}, f32[56,512]{1,0:T(8,128)S(1)}, u32[]{:S(2)}, u32[]{:S(2)}) %collective-permute-start.32) | collective-permute-done | bytes 114720 | tf_op jit(solution)/shard_map/ppermute | solution.py:729
  249.9 3.2 collective-permute-done.31.refs_5_
  253.8 2.2 collective-permute-start.34
  258.6 8.0 %collective-permute-done.33.refs_1_ = bf16[256,512]{1,0:T(8,128)(2,1)S(1)} collective-permute-done((bf16[256,512]{1,0:T(8,128)(2,1)S(1)}, bf16[256,512]{1,0:T(8,128)(2,1)S(1)}, u32[]{:S(2)}, u32[]{:S(2)}) %collective-permute-start.33) | collective-permute-done | bytes 262176 | tf_op jit(solution)/shard_map/ppermute | solution.py:729
  270.4 2.1 collective-permute-start.39
  272.5 9.9 %collective-permute-done.37.refs_1_ = bf16[512,512]{1,0:T(8,128)(2,1)S(1)} collective-permute-done((bf16[512,512]{1,0:T(8,128)(2,1)S(1)}, bf16[512,512]{1,0:T(8,128)(2,1)S(1)}, u32[]{:S(2)}, u32[]{:S(2)}) %collective-permute-start.37) | collective-permute-done | bytes 524320 | tf_op jit(solution)/shard_map/ppermute | solution.py:729
  283.5 2.4 shard_map.376
  293.0 4.8 %shard_map.377 = (f32[2,512,2048]{2,1,0:T(8,128)}, f32[2,2048,512]{2,1,0:T(8,128)}, f32[512,1024]{1,0:T(8,128)}, f32[512,512]{1,0:T(8,128)}, f32[512,512]{1,0:T(8,128)}, /*index=5*/f32[4,512,512]{2,1,0:T(8,128)}) custom-call(s32[4]{0:T(128)} %add_add_fusion.1.places, bf16[1024,512]{1,0:T(8,128)(2,1)} %get-tuple-element.417.refs_0_, ...), custom_call_target="tpu_custom_call" | custom-call | bytes 9437184 | tf_op jit(solution)/shard_map/pallas_call | solution.py:1096
  300.1 4.9 %shard_map.378 = (f32[2,512,2048]{2,1,0:T(8,128)}, f32[2,2048,512]{2,1,0:T(8,128)}, f32[512,1024]{1,0:T(8,128)}, f32[512,512]{1,0:T(8,128)}, f32[512,512]{1,0:T(8,128)}, /*index=5*/f32[4,512,512]{2,1,0:T(8,128)}) custom-call(s32[4]{0:T(128)} %add_add_fusion.2.places, ...), custom_call_target="tpu_custom_call", output_to_operand_aliasing={{0}: (7, {}), {1}: (8, {}), {2}: (9, {}), {3}: (10, {}), {4... | custom-call | bytes 9437184 | tf_op jit(solution)/shard_map/pallas_call | solution.py:1096
  304.9 7.3 %collective-permute-done.43.refs_0_ = bf16[1024,512]{1,0:T(8,128)(2,1)} collective-permute-done((bf16[1024,512]{1,0:T(8,128)(2,1)}, bf16[1024,512]{1,0:T(8,128)(2,1)}, u32[]{:S(2)}, u32[]{:S(2)}) %collective-permute-start.43) | collective-permute-done | bytes 1048608 | tf_op jit(solution)/shard_map/ppermute | solution.py:729
  315.5 4.8 %shard_map.380 = (f32[2,512,2048]{2,1,0:T(8,128)}, f32[2,2048,512]{2,1,0:T(8,128)}, f32[512,1024]{1,0:T(8,128)}, f32[512,512]{1,0:T(8,128)}, f32[512,512]{1,0:T(8,128)}, /*index=5*/f32[4,512,512]{2,1,0:T(8,128)}) custom-call(s32[4]{0:T(128)} %get-tuple-element.488.places, ...), custom_call_target="tpu_custom_call", output_to_operand_aliasing={{0}: (7, {}), {1}: (8, {}), {2}: (9, {}), {3}: (10, {}), {4... | custom-call | bytes 9437184 | tf_op jit(solution)/shard_map/pallas_call | solution.py:1096
  320.4 4.9 %shard_map.381 = (f32[2,512,2048]{2,1,0:T(8,128)}, f32[2,2048,512]{2,1,0:T(8,128)}, f32[512,1024]{1,0:T(8,128)}, f32[512,512]{1,0:T(8,128)}, f32[512,512]{1,0:T(8,128)}, /*index=5*/f32[4,512,512]{2,1,0:T(8,128)}) custom-call(s32[4]{0:T(128)} %get-tuple-element.489.places, ...), custom_call_target="tpu_custom_call", output_to_operand_aliasing={{0}: (7, {}), {1}: (8, {}), {2}: (9, {}), {3}: (10, {}), {4... | custom-call | bytes 9437184 | tf_op jit(solution)/shard_map/pallas_call | solution.py:1096
  (209 shorter events, 79.5 us)
Async XLA Ops:
  7.7 28.2 %all-to-all-start = ((bf16[8,128,384]{2,1,0:T(8,128)(2,1)}), bf16[8,128,384]{2,1,0:T(8,128)(2,1)S(1)}, u32[]{:S(2)}, u32[]{:S(2)}) async-start(bf16[8,128,384]{2,1,0:T(8,128)(2,1)} %get-tuple-element.251), calls=%async_computation | async-start | bytes 1572864 | tf_op jit(solution)/shard_map/all_to_all | solution.py:1131
  15.0 10.0 %collective-permute-start = (f32[2,16,512]{2,1,0:T(8,128)}, f32[2,16,512]{2,1,0:T(8,128)S(1)}, u32[]{:S(2)}, u32[]{:S(2)}) collective-permute-start(f32[2,16,512]{2,1,0:T(8,128)} %get-tuple-element.252), channel_id=1, source_target_pairs={{0,1},{1,2},{2,3},{3,4},{4,5},{5,6},{6,7},{8,9},{9,10},{10,11},{11... | collective-permute-start | bytes 196616 | tf_op jit(solution)/shard_map/ppermute | solution.py:896
  18.9 7.2 %collective-permute-start.1 = (f32[2,16,512]{2,1,0:T(8,128)}, f32[2,16,512]{2,1,0:T(8,128)S(1)}, u32[]{:S(2)}, u32[]{:S(2)}) collective-permute-start(f32[2,16,512]{2,1,0:T(8,128)} %get-tuple-element.253), channel_id=1, source_target_pairs={{1,0},{2,1},{3,2},{4,3},{5,4},{6,5},{7,6},{9,8},{10,9},{11,10},{12... | collective-permute-start | bytes 196616 | tf_op jit(solution)/shard_map/ppermute | solution.py:897
  48.7 18.6 %all-to-all-start.1 = ((bf16[8,144,128]{2,1,0:T(8,128)(2,1)}), bf16[8,144,128]{2,1,0:T(8,128)(2,1)S(1)}, u32[]{:S(2)}, u32[]{:S(2)}) async-start(bf16[8,144,128]{2,1,0:T(8,128)(2,1)} %get-tuple-element.258), calls=%async_computation.1 | async-start | bytes 589824 | tf_op jit(solution)/shard_map/all_to_all | solution.py:1556
  72.8 11.4 %all-to-all-start.2 = ((f32[32,8,128]{2,1,0:T(8,128)}), f32[32,8,128]{2,1,0:T(8,128)S(1)}, u32[]{:S(2)}, u32[]{:S(2)}) async-start(f32[32,8,128]{2,1,0:T(8,128)} %bitcast.65), calls=%async_computation.2 | async-start | bytes 262144 | tf_op jit(solution)/shard_map/all_to_all | solution.py:891
  94.5 6.1 %collective-permute-start.2 = (bf16[256,6144]{1,0:T(8,128)(2,1)}, bf16[256,6144]{1,0:T(8,128)(2,1)}, u32[]{:S(2)}, u32[]{:S(2)}) collective-permute-start(bf16[256,6144]{1,0:T(8,128)(2,1)} %get-tuple-element.289.refs_0_.refs_2_.refs_4_.refs_6_), channel_id=1, source_target_pairs={{0,8},{8,0},{16,24},{24,16},{1,9},{9,1},{17,25},{25,17},{2,10},{10... | collective-permute-start | bytes 9437192 | tf_op jit(solution)/shard_map/ppermute | solution.py:729
  94.6 11.8 %all-to-all-start.3 = ((f32[32,8,128]{2,1,0:T(8,128)}), f32[32,8,128]{2,1,0:T(8,128)S(1)}, u32[]{:S(2)}, u32[]{:S(2)}) async-start(f32[32,8,128]{2,1,0:T(8,128)} %bitcast.64), calls=%async_computation.3 | async-start | bytes 262144 | tf_op jit(solution)/shard_map/all_to_all | solution.py:891
  113.0 7.5 %collective-permute-start.4 = (bf16[256,1536]{1,0:T(8,128)(2,1)}, bf16[256,1536]{1,0:T(8,128)(2,1)S(1)}, u32[]{:S(2)}, u32[]{:S(2)}) collective-permute-start(bf16[256,1536]{1,0:T(8,128)(2,1)} %get-tuple-element.288.refs_2_.refs_10_), channel_id=1, source_target_pairs={{0,8},{8,0},{16,24},{24,16},{1,9},{9,1},{17,25},{25,17},{2,10},{10... | collective-permute-start | bytes 2359304 | tf_op jit(solution)/shard_map/ppermute | solution.py:729
  113.1 7.4 %collective-permute-start.3 = (bf16[256,1024]{1,0:T(8,128)(2,1)}, bf16[256,1024]{1,0:T(8,128)(2,1)}, u32[]{:S(2)}, u32[]{:S(2)}) collective-permute-start(bf16[256,1024]{1,0:T(8,128)(2,1)} %get-tuple-element.287.refs_0_.refs_8_), channel_id=1, source_target_pairs={{0,8},{8,0},{16,24},{24,16},{1,9},{9,1},{17,25},{25,17},{2,10},{10... | collective-permute-start | bytes 1572872 | tf_op jit(solution)/shard_map/ppermute | solution.py:729
  113.5 13.9 %all-to-all-start.4 = ((bf16[8,128,128]{2,1,0:T(8,128)(2,1)}), bf16[8,128,128]{2,1,0:T(8,128)(2,1)}, u32[]{:S(2)}, u32[]{:S(2)}) async-start(bf16[8,128,128]{2,1,0:T(8,128)(2,1)} %get-tuple-element.284), calls=%async_computation.4 | async-start | bytes 524288 | tf_op jit(solution)/shard_map/all_to_all | solution.py:1131
  117.5 22.7 %collective-permute-start.5 = (bf16[512,512]{1,0:T(8,128)(2,1)}, bf16[512,512]{1,0:T(8,128)(2,1)}, u32[]{:S(2)}, u32[]{:S(2)}) collective-permute-start(bf16[512,512]{1,0:T(8,128)(2,1)} %get-tuple-element.296), channel_id=1, source_target_pairs={{0,1},{1,0},{2,3},{3,2},{4,5},{5,4},{6,7},{7,6},{8,9},{9,8},{10,11... | collective-permute-start | bytes 1572872 | tf_op jit(solution)/shard_map/ppermute | solution.py:729
  119.4 20.8 %collective-permute-start.6 = (bf16[512,512]{1,0:T(8,128)(2,1)}, bf16[512,512]{1,0:T(8,128)(2,1)}, u32[]{:S(2)}, u32[]{:S(2)}) collective-permute-start(bf16[512,512]{1,0:T(8,128)(2,1)} %get-tuple-element.297), channel_id=1, source_target_pairs={{0,16},{8,24},{16,0},{24,8},{1,17},{9,25},{17,1},{25,9},{2,18},{10... | collective-permute-start | bytes 1572872 | tf_op jit(solution)/shard_map/ppermute | solution.py:729
  125.9 14.4 %collective-permute-start.7 = (bf16[512,512]{1,0:T(8,128)(2,1)}, bf16[512,512]{1,0:T(8,128)(2,1)}, u32[]{:S(2)}, u32[]{:S(2)}) collective-permute-start(bf16[512,512]{1,0:T(8,128)(2,1)} %get-tuple-element.298), channel_id=1, source_target_pairs={{0,2},{1,3},{2,0},{3,1},{4,6},{5,7},{6,4},{7,5},{8,10},{9,11},{10,... | collective-permute-start | bytes 1572872 | tf_op jit(solution)/shard_map/ppermute | solution.py:729
  127.3 30.4 %collective-permute-start.11 = (bf16[256,3072]{1,0:T(8,128)(2,1)}, bf16[256,3072]{1,0:T(8,128)(2,1)}, u32[]{:S(2)}, u32[]{:S(2)}) collective-permute-start(bf16[256,3072]{1,0:T(8,128)(2,1)} %get-tuple-element.312.refs_0_.refs_2_.refs_4_), channel_id=1, source_target_pairs={{0,8},{8,0},{16,24},{24,16},{1,9},{9,1},{17,25},{25,17},{2,10},{10... | collective-permute-start | bytes 4718600 | tf_op jit(solution)/shard_map/ppermute | solution.py:729
  140.3 26.6 %all-to-all-start.5 = ((bf16[8,128,384]{2,1,0:T(8,128)(2,1)}), bf16[8,128,384]{2,1,0:T(8,128)(2,1)}, u32[]{:S(2)}, u32[]{:S(2)}) async-start(bf16[8,128,384]{2,1,0:T(8,128)(2,1)} %bitcast.55), calls=%async_computation.5 | async-start | bytes 1572864 | tf_op jit(solution)/shard_map/all_to_all | solution.py:1738
  146.1 11.6 %collective-permute-start.12 = (bf16[512,512]{1,0:T(8,128)(2,1)S(1)}, bf16[512,512]{1,0:T(8,128)(2,1)}, u32[]{:S(2)}, u32[]{:S(2)}) collective-permute-start(bf16[512,512]{1,0:T(8,128)(2,1)S(1)} %dynamic_update_slice.6.refs_6_), channel_id=1, source_target_pairs={{0,8},{8,0},{16,24},{24,16},{1,9},{9,1},{17,25},{25,17},{2,10},{10... | collective-permute-start | bytes 1572872 | tf_op jit(solution)/shard_map/ppermute | solution.py:729
  153.3 8.8 %collective-permute-start.8 = (bf16[256,512]{1,0:T(8,128)(2,1)}, bf16[256,512]{1,0:T(8,128)(2,1)S(1)}, u32[]{:S(2)}, u32[]{:S(2)}) collective-permute-start(bf16[256,512]{1,0:T(8,128)(2,1)} %get-tuple-element.309), channel_id=1, source_target_pairs={{0,16},{8,24},{16,0},{24,8},{1,17},{9,25},{17,1},{25,9},{2,18},{10... | collective-permute-start | bytes 786440 | tf_op jit(solution)/shard_map/ppermute | solution.py:729
  154.2 12.7 %collective-permute-start.9 = (bf16[256,512]{1,0:T(8,128)(2,1)}, bf16[256,512]{1,0:T(8,128)(2,1)S(1)}, u32[]{:S(2)}, u32[]{:S(2)}) collective-permute-start(bf16[256,512]{1,0:T(8,128)(2,1)} %get-tuple-element.310), channel_id=1, source_target_pairs={{0,2},{1,3},{2,0},{3,1},{4,6},{5,7},{6,4},{7,5},{8,10},{9,11},{10,... | collective-permute-start | bytes 786440 | tf_op jit(solution)/shard_map/ppermute | solution.py:729
  155.8 11.0 %collective-permute-start.10 = (bf16[256,512]{1,0:T(8,128)(2,1)}, bf16[256,512]{1,0:T(8,128)(2,1)}, u32[]{:S(2)}, u32[]{:S(2)}) collective-permute-start(bf16[256,512]{1,0:T(8,128)(2,1)} %get-tuple-element.311), channel_id=1, source_target_pairs={{0,1},{1,0},{2,3},{3,2},{4,5},{5,4},{6,7},{7,6},{8,9},{9,8},{10,11... | collective-permute-start | bytes 786440 | tf_op jit(solution)/shard_map/ppermute | solution.py:729
  183.7 14.1 %collective-permute-start.14 = (bf16[512,512]{1,0:T(8,128)(2,1)}, bf16[512,512]{1,0:T(8,128)(2,1)S(1)}, u32[]{:S(2)}, u32[]{:S(2)}) collective-permute-start(bf16[512,512]{1,0:T(8,128)(2,1)} %get-tuple-element.342), channel_id=1, source_target_pairs={{0,1},{1,0},{2,3},{3,2},{4,5},{5,4},{6,7},{7,6},{8,9},{9,8},{10,11... | collective-permute-start | bytes 1572872 | tf_op jit(solution)/shard_map/ppermute | solution.py:729
  185.7 13.5 %collective-permute-start.15 = (bf16[512,512]{1,0:T(8,128)(2,1)}, bf16[512,512]{1,0:T(8,128)(2,1)S(1)}, u32[]{:S(2)}, u32[]{:S(2)}) collective-permute-start(bf16[512,512]{1,0:T(8,128)(2,1)} %get-tuple-element.343), channel_id=1, source_target_pairs={{0,16},{8,24},{16,0},{24,8},{1,17},{9,25},{17,1},{25,9},{2,18},{10... | collective-permute-start | bytes 1572872 | tf_op jit(solution)/shard_map/ppermute | solution.py:729
  186.7 13.2 %collective-permute-start.16 = (bf16[512,512]{1,0:T(8,128)(2,1)}, bf16[512,512]{1,0:T(8,128)(2,1)S(1)}, u32[]{:S(2)}, u32[]{:S(2)}) collective-permute-start(bf16[512,512]{1,0:T(8,128)(2,1)} %get-tuple-element.344), channel_id=1, source_target_pairs={{0,2},{1,3},{2,0},{3,1},{4,6},{5,7},{6,4},{7,5},{8,10},{9,11},{10,... | collective-permute-start | bytes 1572872 | tf_op jit(solution)/shard_map/ppermute | solution.py:729
  200.8 8.6 %collective-permute-start.17 = (bf16[256,512]{1,0:T(8,128)(2,1)S(1)}, bf16[256,512]{1,0:T(8,128)(2,1)S(1)}, u32[]{:S(2)}, u32[]{:S(2)}) collective-permute-start(bf16[256,512]{1,0:T(8,128)(2,1)S(1)} %get-tuple-element.358), channel_id=1, source_target_pairs={{0,16},{8,24},{16,0},{24,8},{1,17},{9,25},{17,1},{25,9},{2,18},{10... | collective-permute-start | bytes 786440 | tf_op jit(solution)/shard_map/ppermute | solution.py:729
  201.9 8.6 %collective-permute-start.18 = (bf16[256,512]{1,0:T(8,128)(2,1)S(1)}, bf16[256,512]{1,0:T(8,128)(2,1)S(1)}, u32[]{:S(2)}, u32[]{:S(2)}) collective-permute-start(bf16[256,512]{1,0:T(8,128)(2,1)S(1)} %get-tuple-element.359), channel_id=1, source_target_pairs={{0,2},{1,3},{2,0},{3,1},{4,6},{5,7},{6,4},{7,5},{8,10},{9,11},{10,... | collective-permute-start | bytes 786440 | tf_op jit(solution)/shard_map/ppermute | solution.py:729
  202.2 8.4 %collective-permute-start.19 = (bf16[256,512]{1,0:T(8,128)(2,1)S(1)}, bf16[256,512]{1,0:T(8,128)(2,1)S(1)}, u32[]{:S(2)}, u32[]{:S(2)}) collective-permute-start(bf16[256,512]{1,0:T(8,128)(2,1)S(1)} %get-tuple-element.360), channel_id=1, source_target_pairs={{0,1},{1,0},{2,3},{3,2},{4,5},{5,4},{6,7},{7,6},{8,9},{9,8},{10,11... | collective-permute-start | bytes 786440 | tf_op jit(solution)/shard_map/ppermute | solution.py:729
  202.9 6.6 %collective-permute-start.20 = (f32[56,512]{1,0:T(8,128)S(1)}, f32[56,512]{1,0:T(8,128)S(1)}, u32[]{:S(2)}, u32[]{:S(2)}) collective-permute-start(f32[56,512]{1,0:T(8,128)S(1)} %pad_maximum_fusion.1), channel_id=1, source_target_pairs={{0,4},{1,5},{2,6},{3,7},{4,0},{5,1},{6,2},{7,3},{8,12},{9,13},{10,... | collective-permute-start | bytes 344072 | tf_op jit(solution)/shard_map/ppermute | solution.py:729
  212.4 13.1 %collective-permute-start.21 = (bf16[256,512]{1,0:T(8,128)(2,1)S(1)}, bf16[256,512]{1,0:T(8,128)(2,1)S(1)}, u32[]{:S(2)}, u32[]{:S(2)}) collective-permute-start(bf16[256,512]{1,0:T(8,128)(2,1)S(1)} %get-tuple-element.375), channel_id=1, source_target_pairs={{0,2},{1,3},{2,0},{3,1},{4,6},{5,7},{6,4},{7,5},{8,10},{9,11},{10,... | collective-permute-start | bytes 786440 | tf_op jit(solution)/shard_map/ppermute | solution.py:729
  213.9 11.7 %collective-permute-start.22 = (bf16[256,512]{1,0:T(8,128)(2,1)S(1)}, bf16[256,512]{1,0:T(8,128)(2,1)S(1)}, u32[]{:S(2)}, u32[]{:S(2)}) collective-permute-start(bf16[256,512]{1,0:T(8,128)(2,1)S(1)} %get-tuple-element.376), channel_id=1, source_target_pairs={{0,4},{1,5},{2,6},{3,7},{4,0},{5,1},{6,2},{7,3},{8,12},{9,13},{10,... | collective-permute-start | bytes 786440 | tf_op jit(solution)/shard_map/ppermute | solution.py:729
  215.6 9.9 %collective-permute-start.23 = (bf16[256,512]{1,0:T(8,128)(2,1)S(1)}, bf16[256,512]{1,0:T(8,128)(2,1)S(1)}, u32[]{:S(2)}, u32[]{:S(2)}) collective-permute-start(bf16[256,512]{1,0:T(8,128)(2,1)S(1)} %get-tuple-element.377), channel_id=1, source_target_pairs={{0,16},{8,24},{16,0},{24,8},{1,17},{9,25},{17,1},{25,9},{2,18},{10... | collective-permute-start | bytes 786440 | tf_op jit(solution)/shard_map/ppermute | solution.py:729
  216.7 8.9 %collective-permute-start.24 = (f32[56,512]{1,0:T(8,128)S(1)}, f32[56,512]{1,0:T(8,128)S(1)}, u32[]{:S(2)}, u32[]{:S(2)}) collective-permute-start(f32[56,512]{1,0:T(8,128)S(1)} %add.95), channel_id=1, source_target_pairs={{0,2},{1,3},{2,0},{3,1},{4,6},{5,7},{6,4},{7,5},{8,10},{9,11},{10,... | collective-permute-start | bytes 344072 | tf_op jit(solution)/shard_map/ppermute | solution.py:729
  226.3 10.1 %collective-permute-start.25 = (bf16[128,512]{1,0:T(8,128)(2,1)S(1)}, bf16[128,512]{1,0:T(8,128)(2,1)S(1)}, u32[]{:S(2)}, u32[]{:S(2)}) collective-permute-start(bf16[128,512]{1,0:T(8,128)(2,1)S(1)} %get-tuple-element.388), channel_id=1, source_target_pairs={{0,4},{1,5},{2,6},{3,7},{4,0},{5,1},{6,2},{7,3},{8,12},{9,13},{10,... | collective-permute-start | bytes 393224 | tf_op jit(solution)/shard_map/ppermute | solution.py:729
  228.7 7.6 %collective-permute-start.26 = (bf16[128,512]{1,0:T(8,128)(2,1)S(1)}, bf16[128,512]{1,0:T(8,128)(2,1)S(1)}, u32[]{:S(2)}, u32[]{:S(2)}) collective-permute-start(bf16[128,512]{1,0:T(8,128)(2,1)S(1)} %get-tuple-element.389), channel_id=1, source_target_pairs={{0,1},{1,0},{2,3},{3,2},{4,5},{5,4},{6,7},{7,6},{8,9},{9,8},{10,11... | collective-permute-start | bytes 393224 | tf_op jit(solution)/shard_map/ppermute | solution.py:729
  231.1 8.1 %collective-permute-start.27 = (bf16[128,512]{1,0:T(8,128)(2,1)S(1)}, bf16[128,512]{1,0:T(8,128)(2,1)S(1)}, u32[]{:S(2)}, u32[]{:S(2)}) collective-permute-start(bf16[128,512]{1,0:T(8,128)(2,1)S(1)} %get-tuple-element.390), channel_id=1, source_target_pairs={{0,4},{1,5},{2,6},{3,7},{4,0},{5,1},{6,2},{7,3},{8,12},{9,13},{10,... | collective-permute-start | bytes 393224 | tf_op jit(solution)/shard_map/ppermute | solution.py:729
  239.3 10.6 %collective-permute-start.29 = (bf16[128,512]{1,0:T(8,128)(2,1)S(1)}, bf16[128,512]{1,0:T(8,128)(2,1)S(1)}, u32[]{:S(2)}, u32[]{:S(2)}) collective-permute-start(bf16[128,512]{1,0:T(8,128)(2,1)S(1)} %get-tuple-element.397.refs_0_), channel_id=1, source_target_pairs={{0,4},{1,5},{2,6},{3,7},{4,0},{5,1},{6,2},{7,3},{8,12},{9,13},{10,... | collective-permute-start | bytes 393224 | tf_op jit(solution)/shard_map/ppermute | solution.py:729
  239.4 10.5 %collective-permute-start.30 = (bf16[128,512]{1,0:T(8,128)(2,1)S(1)}, bf16[128,512]{1,0:T(8,128)(2,1)S(1)}, u32[]{:S(2)}, u32[]{:S(2)}) collective-permute-start(bf16[128,512]{1,0:T(8,128)(2,1)S(1)} %get-tuple-element.398.refs_2_), channel_id=1, source_target_pairs={{0,1},{1,0},{2,3},{3,2},{4,5},{5,4},{6,7},{7,6},{8,9},{9,8},{10,11... | collective-permute-start | bytes 393224 | tf_op jit(solution)/shard_map/ppermute | solution.py:729
  242.2 10.9 %collective-permute-start.31 = (bf16[128,512]{1,0:T(8,128)(2,1)S(1)}, bf16[128,512]{1,0:T(8,128)(2,1)S(1)}, u32[]{:S(2)}, u32[]{:S(2)}) collective-permute-start(bf16[128,512]{1,0:T(8,128)(2,1)S(1)} %get-tuple-element.399.refs_4_), channel_id=1, source_target_pairs={{0,4},{1,5},{2,6},{3,7},{4,0},{5,1},{6,2},{7,3},{8,12},{9,13},{10,... | collective-permute-start | bytes 393224 | tf_op jit(solution)/shard_map/ppermute | solution.py:729
  253.7 12.9 %collective-permute-start.33 = (bf16[256,512]{1,0:T(8,128)(2,1)S(1)}, bf16[256,512]{1,0:T(8,128)(2,1)S(1)}, u32[]{:S(2)}, u32[]{:S(2)}) collective-permute-start(bf16[256,512]{1,0:T(8,128)(2,1)S(1)} %get-tuple-element.404.refs_0_), channel_id=1, source_target_pairs={{0,2},{1,3},{2,0},{3,1},{4,6},{5,7},{6,4},{7,5},{8,10},{9,11},{10,... | collective-permute-start | bytes 786440 | tf_op jit(solution)/shard_map/ppermute | solution.py:729
  253.8 14.9 %collective-permute-start.34 = (bf16[256,512]{1,0:T(8,128)(2,1)S(1)}, bf16[256,512]{1,0:T(8,128)(2,1)S(1)}, u32[]{:S(2)}, u32[]{:S(2)}) collective-permute-start(bf16[256,512]{1,0:T(8,128)(2,1)S(1)} %get-tuple-element.405.refs_2_), channel_id=1, source_target_pairs={{0,4},{1,5},{2,6},{3,7},{4,0},{5,1},{6,2},{7,3},{8,12},{9,13},{10,... | collective-permute-start | bytes 786440 | tf_op jit(solution)/shard_map/ppermute | solution.py:729
  256.0 12.7 %collective-permute-start.35 = (bf16[256,512]{1,0:T(8,128)(2,1)S(1)}, bf16[256,512]{1,0:T(8,128)(2,1)S(1)}, u32[]{:S(2)}, u32[]{:S(2)}) collective-permute-start(bf16[256,512]{1,0:T(8,128)(2,1)S(1)} %get-tuple-element.406.refs_4_), channel_id=1, source_target_pairs={{0,16},{8,24},{16,0},{24,8},{1,17},{9,25},{17,1},{25,9},{2,18},{10... | collective-permute-start | bytes 786440 | tf_op jit(solution)/shard_map/ppermute | solution.py:729
  269.3 13.1 %collective-permute-start.37 = (bf16[512,512]{1,0:T(8,128)(2,1)S(1)}, bf16[512,512]{1,0:T(8,128)(2,1)S(1)}, u32[]{:S(2)}, u32[]{:S(2)}) collective-permute-start(bf16[512,512]{1,0:T(8,128)(2,1)S(1)} %get-tuple-element.411.refs_0_), channel_id=1, source_target_pairs={{0,16},{8,24},{16,0},{24,8},{1,17},{9,25},{17,1},{25,9},{2,18},{10... | collective-permute-start | bytes 1572872 | tf_op jit(solution)/shard_map/ppermute | solution.py:729
  270.4 12.1 %collective-permute-start.38 = (bf16[512,512]{1,0:T(8,128)(2,1)S(1)}, bf16[512,512]{1,0:T(8,128)(2,1)S(1)}, u32[]{:S(2)}, u32[]{:S(2)}) collective-permute-start(bf16[512,512]{1,0:T(8,128)(2,1)S(1)} %get-tuple-element.412.refs_2_), channel_id=1, source_target_pairs={{0,2},{1,3},{2,0},{3,1},{4,6},{5,7},{6,4},{7,5},{8,10},{9,11},{10,... | collective-permute-start | bytes 1572872 | tf_op jit(solution)/shard_map/ppermute | solution.py:729
  270.4 13.1 %collective-permute-start.39 = (bf16[512,512]{1,0:T(8,128)(2,1)S(1)}, bf16[512,512]{1,0:T(8,128)(2,1)S(1)}, u32[]{:S(2)}, u32[]{:S(2)}) collective-permute-start(bf16[512,512]{1,0:T(8,128)(2,1)S(1)} %get-tuple-element.413.refs_4_), channel_id=1, source_target_pairs={{0,1},{1,0},{2,3},{3,2},{4,5},{5,4},{6,7},{7,6},{8,9},{9,8},{10,11... | collective-permute-start | bytes 1572872 | tf_op jit(solution)/shard_map/ppermute | solution.py:729
  285.9 14.2 %collective-permute-start.41 = (bf16[1024,512]{1,0:T(8,128)(2,1)}, bf16[1024,512]{1,0:T(8,128)(2,1)}, u32[]{:S(2)}, u32[]{:S(2)}) collective-permute-start(bf16[1024,512]{1,0:T(8,128)(2,1)} %get-tuple-element.418.refs_1_), channel_id=1, source_target_pairs={{0,8},{8,0},{16,24},{24,16},{1,9},{9,1},{17,25},{25,17},{2,10},{10... | collective-permute-start | bytes 3145736 | tf_op jit(solution)/shard_map/ppermute | solution.py:729
  286.4 13.7 %collective-permute-start.42 = (bf16[1024,512]{1,0:T(8,128)(2,1)}, bf16[1024,512]{1,0:T(8,128)(2,1)}, u32[]{:S(2)}, u32[]{:S(2)}) collective-permute-start(bf16[1024,512]{1,0:T(8,128)(2,1)} %get-tuple-element.419.refs_2_.refs_3_.refs_4_.refs_5_), channel_id=1, source_target_pairs={{0,8},{8,0},{16,24},{24,16},{1,9},{9,1},{17,25},{25,17},{2,10},{10... | collective-permute-start | bytes 3145736 | tf_op jit(solution)/shard_map/ppermute | solution.py:729
  286.4 25.9 %collective-permute-start.43 = (bf16[1024,512]{1,0:T(8,128)(2,1)}, bf16[1024,512]{1,0:T(8,128)(2,1)}, u32[]{:S(2)}, u32[]{:S(2)}) collective-permute-start(bf16[1024,512]{1,0:T(8,128)(2,1)} %get-tuple-element.417.refs_0_), channel_id=1, source_target_pairs={{0,1},{1,0},{2,3},{3,2},{4,5},{5,4},{6,7},{7,6},{8,9},{9,8},{10,11... | collective-permute-start | bytes 3145736 | tf_op jit(solution)/shard_map/ppermute | solution.py:729
  288.1 25.6 %collective-permute-start.44 = (bf16[1024,512]{1,0:T(8,128)(2,1)}, bf16[1024,512]{1,0:T(8,128)(2,1)}, u32[]{:S(2)}, u32[]{:S(2)}) collective-permute-start(bf16[1024,512]{1,0:T(8,128)(2,1)} %get-tuple-element.418.refs_1_), channel_id=1, source_target_pairs={{0,16},{8,24},{16,0},{24,8},{1,17},{9,25},{17,1},{25,9},{2,18},{10... | collective-permute-start | bytes 3145736 | tf_op jit(solution)/shard_map/ppermute | solution.py:729
  289.1 25.3 %collective-permute-start.45 = (bf16[1024,512]{1,0:T(8,128)(2,1)}, bf16[1024,512]{1,0:T(8,128)(2,1)}, u32[]{:S(2)}, u32[]{:S(2)}) collective-permute-start(bf16[1024,512]{1,0:T(8,128)(2,1)} %get-tuple-element.419.refs_2_.refs_3_.refs_4_.refs_5_), channel_id=1, source_target_pairs={{0,2},{1,3},{2,0},{3,1},{4,6},{5,7},{6,4},{7,5},{8,10},{9,11},{10,... | collective-permute-start | bytes 3145736 | tf_op jit(solution)/shard_map/ppermute | solution.py:729
  314.4 6.0 %collective-permute-start.47 = (bf16[1024,512]{1,0:T(8,128)(2,1)}, bf16[1024,512]{1,0:T(8,128)(2,1)}, u32[]{:S(2)}, u32[]{:S(2)}) collective-permute-start(bf16[1024,512]{1,0:T(8,128)(2,1)} %collective-permute-done.44.refs_1_), channel_id=1, source_target_pairs={{0,8},{8,0},{16,24},{24,16},{1,9},{9,1},{17,25},{25,17},{2,10},{10... | collective-permute-start | bytes 3145736 | tf_op jit(solution)/shard_map/ppermute | solution.py:729
  (45 other events, 350.1 us)
where the time goes:
time: 327 us; the launch traced here: 325 us
  Pallas kernels  118 us (36%)
  waiting for transfers between devices  88.2 us (27%)
  starting transfers between devices  82.3 us (25%)
  local copies, waits for them, and re-layouts  23.1 us (7%)
  other arithmetic  5.98 us (2%)
  blocking collectives  5.43 us (2%)
    ppermute x47, waiting for transfers between devices, swap(): lax.ppermute(values, axis, [(i, i ^ mask) for i in range(lax.axis_size(ax...  74.2 us
    pallas_call x10, Pallas kernels, vmem_call(): pl.pallas_call(kernel, grid_spec=pltpu.PrefetchScalarGridSpec(num_scalar_...  55.1 us
    ppermute x47, starting transfers between devices, swap(): lax.ppermute(values, axis, [(i, i ^ mask) for i in range(lax.axis_size(ax...  46.3 us
    pallas_call x4, Pallas kernels, spread_blocks(): pl.pallas_call(functools.partial(spread_kernel, len(pieces)), grid_spec=p...  19.4 us
    unnamed x78, local copies, waits for them, and re-layouts  15.2 us
    pallas_call x1, Pallas kernels, attend_heads_back(): pl.pallas_call(attend_back_kernel, grid=(query_frames // height,), in_spe...  12.9 us
    pallas_call x1, Pallas kernels, attend_heads(): pl.pallas_call(kernel, grid=(query_frames // height,), in_specs=[pl.Block...  11.8 us
    all_to_all x2, starting transfers between devices, heads_out(): lax.all_to_all(jnp.tile(blocks, (groups, 1, 1)), 'seq', 0, 0, tiled=True)  11.3 us
  transfers between devices with their start and end apart: 55, of which 26 were waited for; matrix products, arithmetic and copies ran while one was open for 4% of the time, Pallas kernels for 17%

commit v1 on v0

--- a/solution.py
+++ b/solution.py
@@ -18,7 +18,6 @@
 EPSILON = 1e-05
 VMEM_LIMIT = 63 * 1024 * 1024
 SUM_LIMIT = 20 * 1024 * 1024
-FOLD_LIMIT = SUM_LIMIT
 HALO = 8
 
 
@@ -386,9 +385,9 @@
     return jnp.concatenate([tile[i : i + 1] for i in range(tile.shape[0])], axis=1)
 
 
-def frame_counts(limits, shape, utterances, seq_count, per):
+def frame_counts(limits, utt_index, shape, utterances, seq_count, per):
     place = lax.broadcasted_iota(jnp.int32, shape, 0)
-    owner, first = place // seq_count, place % seq_count * per
+    owner, first = (place // seq_count) ^ utt_index, place % seq_count * per
     total = jnp.zeros(shape, jnp.int32)
     for number in range(limits.shape[0]):
         inside = jnp.clip(limits[number] - first, 0, per)
@@ -400,6 +399,7 @@
     utterances,
     seq_count,
     limits,
+    utt_index,
     convolved,
     shared,
     after,
@@ -441,7 +441,7 @@
     copies = fetch([(feed_in.at[1], weight_in), (feed_out.at[1], weight_out)], semaphores)
     parts = shared[...].reshape(-1, 8, 128)
     per = grads.shape[0] // utterances
-    counts = frame_counts(limits, parts.shape, utterances, seq_count, per)
+    counts = frame_counts(limits, utt_index[0], parts.shape, utterances, seq_count, per)
     totals = jnp.sum(parts, axis=0)
     valid_tile = jnp.sum(counts, axis=0)
     valid = as_row(valid_tile[:4])
@@ -760,7 +760,7 @@
                     first += height
 
 
-def fold_rows(pairs, steps, parts=1):
+def fold_rows(pairs, steps, parts=1, limit=SUM_LIMIT):
     operands = list(zip(*(rows for pair in pairs for rows in pair)))
     heights = [sum(rows.shape[0] for rows in four[::2]) // 2 for four in operands]
     if any(rows.shape[0] // parts % 32 for four in operands for rows in four):
@@ -791,7 +791,7 @@
             out_specs=[whole(height) for height in outs],
         ),
         out_shape=[jax.ShapeDtypeStruct((height, 512), jnp.bfloat16) for height in outs],
-        compiler_params=pltpu.CompilerParams(vmem_limit_bytes=FOLD_LIMIT),
+        compiler_params=pltpu.CompilerParams(vmem_limit_bytes=limit),
         cost_estimate=pl.CostEstimate(
             flops=0, bytes_accessed=6 * 1024 * sum(outs), transcendentals=0
         ),
@@ -1168,6 +1168,7 @@
     held,
 ):
     scale = HEAD_DIM ** (-0.5)
+    weight_rows = jnp.concatenate([weight[...]] * limits.shape[0], axis=0)
     content_rows = content[...]
     key_side = jnp.concatenate([table[...], keys[...]], axis=1)
     places = lax.broadcasted_iota(jnp.int32, (1, table.shape[0]), 1)
@@ -1177,7 +1178,7 @@
         mine = jnp.where(ours, content_rows, jnp.zeros_like(content_rows))
         moved = jnp.where(ours, shift[...], 0.0)
         _, turned_cos, turned_sin = turned_queries(
-            mine, moved, weight[...], sines[...], cosines[...]
+            mine, moved, weight_rows, sines[...], cosines[...]
         )
         query_side = jnp.concatenate([turned_cos, turned_sin, mine], axis=1) * scale
         scores = rows_dot(query_side.astype(jnp.bfloat16), key_side)
@@ -1243,6 +1244,7 @@
         weight_out[...] = jnp.zeros_like(weight_out)
         sums_out[...] = jnp.zeros_like(sums_out)
 
+    weight_rows = jnp.concatenate([weight[...]] * weights.shape[0], axis=0)
     content_rows, grad_rows = content[...], grads[...]
     content_cols = content_rows.T
     grad_cols = grad_rows.T
@@ -1280,7 +1282,7 @@
             offset.T[low:high, :], from_table, preferred_element_type=jnp.float32
         )
         content_part = grad_side[:, 2 * half :]
-        position_part = rows_dot(from_table, weight[...])
+        position_part = rows_dot(from_table, weight_rows)
         if grad_content is None:
             grad_content, grad_position = content_part, position_part
         else:
@@ -1487,18 +1489,12 @@
         cost=row_flops * (2 * hidden_units + 3 * features),
         held=(feed_in, feed_out, attend_in),
     )
-    sent, edge_head, edge_tail = tie(sent, edge_head, edge_tail)
+    sent, all_limits, edge_head, edge_tail = tie(sent, lengths, edge_head, edge_tail)
     before, behind = from_neighbours(edge_head, edge_tail)
-    after_sides, grad_sides = vmem_call(
-        sides_kernel,
-        [((2 * utt_rows * HALO, features), f32)] * 2,
-        (),
-        (before, behind, norm_gain, norm_bias, feed_in_bias, feed_out_bias),
-        scratch=feed_scratch + [pltpu.SemaphoreType.DMA((2,))],
-        cost=row_flops * 2 * hidden_units // 4,
-        held=(feed_in, feed_out),
-    )
-    arrived, after_sides, grad_sides = tie(heads_out(sent, groups), after_sides, grad_sides)
+    arrived = heads_out(sent, groups)
+    for step in axis_bits("utt"):
+        all_limits = jnp.concatenate([all_limits, swap(all_limits, step)])
+    arrived, all_limits = tie(arrived, all_limits)
     arrived = arrived.reshape(frames_all, 3 * lanes)
     start_query = group * query_frames
     head_content = arrived
@@ -1511,9 +1507,7 @@
     head_weight = lax.dynamic_slice_in_dim(attend_in[3], head * HEAD_DIM, HEAD_DIM, 1).reshape(
         features // 2, 2, HEAD_DIM
     )
-    head_weight = jnp.tile(
-        jnp.transpose(head_weight, (2, 1, 0)).reshape(HEAD_DIM, features), (utt_rows, 1)
-    )
+    head_weight = jnp.transpose(head_weight, (2, 1, 0)).reshape(HEAD_DIM, features)
     sines, cosines = angle_tables(frames_all, features)
     key_table = jnp.concatenate([cosines, sines], axis=1).astype(bf16)
     query_sin = lax.dynamic_slice_in_dim(sines, start_query, query_frames, 0)
@@ -1542,8 +1536,16 @@
         ).reshape(groups, HEADS, block_frames, width)
         return lax.dynamic_slice_in_dim(blocks, group, 1, 0)[0]
 
-    head_attended, own_limits = tie(head_attended, lengths)
-    all_limits = lax.all_gather(own_limits, "utt", tiled=True)
+    head_attended, before, behind = tie(head_attended, before, behind)
+    after_sides, grad_sides = vmem_call(
+        sides_kernel,
+        [((2 * utt_rows * HALO, features), f32)] * 2,
+        (),
+        (before, behind, norm_gain, norm_bias, feed_in_bias, feed_out_bias),
+        scratch=feed_scratch + [pltpu.SemaphoreType.DMA((2,))],
+        cost=row_flops * 2 * hidden_units // 4,
+        held=(feed_in, feed_out),
+    )
     if head_attended.ndim == 2:
         placed = lax.dynamic_update_slice_in_dim(
             jnp.zeros((frames_all + 2 * HALO, lanes), bf16), head_attended, HALO + start_query, 0
@@ -1554,7 +1556,7 @@
         )
         head_attended = jnp.concatenate([main, before[:, :HALO], behind[:, -HALO:]], axis=1)
     attended_blocks = lax.all_to_all(head_attended, "seq", 0, 0, tiled=True)
-    attended_blocks, all_limits = tie(attended_blocks, all_limits)
+    attended_blocks, after_sides, grad_sides = tie(attended_blocks, after_sides, grad_sides)
     if groups > 1:
         attended_blocks = jnp.sum(
             attended_blocks.reshape((groups, HEADS) + attended_blocks.shape[1:]), axis=0
@@ -1618,7 +1620,7 @@
             ((8, features), f32),
             ((16, features), f32),
         ],
-        (all_limits,),
+        (all_limits, lax.axis_index("utt").reshape(1)),
         (
             convolved,
             all_shared(shared),
@@ -1754,7 +1756,7 @@
         1,
     )
     def next_phase(kept, arrived_rows, steps):
-        sent_rows, kept = fold_rows([(kept, arrived_rows)], steps)
+        sent_rows, kept = fold_rows([(kept, arrived_rows)], steps, 1, VMEM_LIMIT)
         return kept, swap_all(tie(sent_rows)[0], steps)
 
     early_kept, early_arrived = next_phase(early_kept, early_arrived, phases[1])
@@ -1809,24 +1811,48 @@
     late_kept = late_blocks(True, places, *late_factors)
     flat = jnp.concatenate([middle_rows, mixer_rows, entry_rows, head_vector_grads], axis=0)
     flat_steps = [near] + [steps[0] for steps in phases]
-    late_arrived, flat = tie(late_arrived, flat)
+    def in_turn(arrived_rows, steps, work):
+        nonlocal flat
+        flat_arrived = swap(flat, flat_steps.pop()) if flat_steps else jnp.zeros_like(flat)
+        after, next_arrived = None, []
+        for i, rows in enumerate(arrived_rows):
+            if after is not None:
+                rows, _ = tie(rows, after)
+            if i == len(arrived_rows) - 1:
+                rows, flat_arrived = tie(rows, flat_arrived)
+            after = work(i, rows)
+            next_arrived.append(swap(after, steps[i]) if steps else after)
+        flat = flat + flat_arrived
+        return next_arrived
+
+    late_kept = list(late_kept)
     for steps in phases[1:]:
-        pairs = [(late_kept, late_arrived)]
-        if steps is phases[2]:
-            pairs = [(early_kept, early_arrived)] + pairs
-        parts = 1 if steps in phases[1:3] else 2
-        sent_rows, late_kept = fold_rows(pairs, steps, parts)
-        (sent_rows,) = tie(sent_rows)
-        late_arrived, flat_arrived = tie(swap_all(sent_rows, steps), swap(flat, flat_steps.pop()))
-        flat = flat + flat_arrived
-    sums = add_rows(late_kept, late_arrived)
-    for steps in phases[:0:-1]:
-        (sums,) = tie(sums)
-        flat_arrived = swap(flat, flat_steps.pop()) if flat_steps else jnp.zeros_like(flat)
-        arrived_rows, flat_arrived = tie(swap_all(sums, steps), flat_arrived)
-        flat = flat + flat_arrived
-        sums = join_rows(sums, arrived_rows, steps)
-    (sums,) = tie(sums)
+
+        def fold(i, rows):
+            pairs = [([late_kept[i]], [rows])]
+            if steps is phases[2]:
+                pairs = [([early_kept[i]], [early_arrived[i]])] + pairs
+            parts = 1 if steps in phases[1:3] else 2
+            (sent_rows,), (late_kept[i],) = fold_rows(pairs, [steps[i]], parts)
+            return sent_rows
+
+        late_arrived = in_turn(late_arrived, steps, fold)
+    sums = [None] * len(late_arrived)
+
+    def add(i, rows):
+        (sums[i],) = add_rows([late_kept[i]], [rows])
+        return sums[i]
+
+    arrived_rows = in_turn(late_arrived, phases[-1], add)
+    for number in range(len(phases) - 1, 0, -1):
+
+        def join(i, rows):
+            (sums[i],) = join_rows([sums[i]], [rows], [phases[number][i]])
+            return sums[i]
+
+        arrived_rows = in_turn(arrived_rows, phases[number - 1], join)
+    for step in flat_steps:
+        flat = flat + swap(flat, step)
     vector_grads = vmem_call(
         vectors_kernel,
         [
@@ -1846,7 +1872,6 @@
     vector_grads[5] = vector_grads[5].reshape(-1)
     vector_grads[7] = vector_grads[7].T
     vector_grads = [*vector_grads, batch_grads[1], batch_grads[0], batch_rows[2], batch_rows[3]]
-    arrived_rows = swap_all(sums, phases[0])
     across_rows = swap_all(sums, [near] * 3)
     shapes = [feed_in.shape, feed_out.shape, mixer_in.shape, mixer_out.shape]
     shapes += [attend_out.shape, attend_in.shape]

time: 327 us -> 312 us (0.954)
  starting transfers between devices: 82.3 us -> 72.9 us
  blocking collectives: 5.43 us -> 0 us
    all_to_all x1, starting transfers between devices: 8.87 us -> 3.43 us  [shards(): attended_blocks = lax.all_to_all(head_attended, 'seq', 0, 0, tiled=True)]
    optimization_barrier x1 -> x0, blocking collectives: 5.43 us -> none  [tie(): return lax.optimization_barrier(groups)]
    ppermute x47 -> x49, starting transfers between devices: 46.3 us -> 42.4 us  [swap(): lax.ppermute(values, axis, [(i, i ^ mask) for i in range(lax.axis_size(ax...]
    ppermute x47 -> x49, waiting for transfers between devices: 74.2 us -> 70.6 us  [swap(): lax.ppermute(values, axis, [(i, i ^ mask) for i in range(lax.axis_size(ax...]
    unnamed x78 -> x69, local copies, waits for them, and re-layouts: 15.2 us -> 13.5 us
    pallas_call x4 -> x10, Pallas kernels: 6.5 us -> 7.17 us  [fold_rows(): pl.pallas_call(functools.partial(fold_kernel, len(steps), len(pairs), par...]
  transfers between devices with their start and end apart: 55 -> 57, of which waited for: 26 -> 22; matrix products, arithmetic and copies ran while one was open for 4% -> 5% of each run, Pallas kernels for 17% -> 23%
where the time goes in v1:
time: 312 us; the launch traced here: 310 us
  Pallas kernels  119 us (38%)
  waiting for transfers between devices  86.9 us (28%)
  starting transfers between devices  72.9 us (23%)
  local copies, waits for them, and re-layouts  22.8 us (7%)
  other arithmetic  7.02 us (2%)
    ppermute x49, waiting for transfers between devices, swap(): lax.ppermute(values, axis, [(i, i ^ mask) for i in range(lax.axis_size(ax...  70.6 us
    pallas_call x10, Pallas kernels, vmem_call(): pl.pallas_call(kernel, grid_spec=pltpu.PrefetchScalarGridSpec(num_scalar_...  55.3 us
    ppermute x49, starting transfers between devices, swap(): lax.ppermute(values, axis, [(i, i ^ mask) for i in range(lax.axis_size(ax...  42.4 us
    pallas_call x4, Pallas kernels, spread_blocks(): pl.pallas_call(functools.partial(spread_kernel, len(pieces)), grid_spec=p...  19.4 us
    unnamed x69, local copies, waits for them, and re-layouts  13.5 us
    pallas_call x1, Pallas kernels, attend_heads_back(): pl.pallas_call(attend_back_kernel, grid=(query_frames // height,), in_spe...  12.8 us
    pallas_call x1, Pallas kernels, attend_heads(): pl.pallas_call(kernel, grid=(query_frames // height,), in_specs=[pl.Block...  11.8 us
    all_to_all x2, starting transfers between devices, heads_out(): lax.all_to_all(jnp.tile(blocks, (groups, 1, 1)), 'seq', 0, 0, tiled=True)  11.3 us
  transfers between devices with their start and end apart: 57, of which 22 were waited for; matrix products, arithmetic and copies ran while one was open for 5% of the time, Pallas kernels for 23%

profile of v1, /device:TPU:0, one launch (start us, length us, event | category | flops | bytes accessed | tf_op | source)
XLA Modules:
  0.0 309.9 jit_solution(5716262218042263984)
XLA Ops:
  0.7 7.1 %shard_map.356 = (f32[2,16,512]{2,1,0:T(8,128)}, f32[2,16,512]{2,1,0:T(8,128)}, f32[256,512]{1,0:T(8,128)}, bf16[256,2048]{1,0:T(8,128)(2,1)}, bf16[256,3072]{1,0:T(8,128)(2,1)}, /*index=5*/bf16[8,128,384]{2,1,0:T(8,128)(2,1)}) custom-call(f32[256,512]{1,0:T(8,128)} %bitcast.46, bf16[5,512]{1,0:T(8,128)(2,1)} %gains.11, bf16[5,512]{1,0:T(8,128)(2,1)} %biases.7, ...), custom_call_target="tpu_custom_call" | custom-call | flops 1476395008 | bytes 4921316 | tf_op jit(solution)/shard_map/pallas_call | solution.py:143
  7.8 7.3 %all-to-all-start = ((bf16[8,128,384]{2,1,0:T(8,128)(2,1)}), bf16[8,128,384]{2,1,0:T(8,128)(2,1)}, u32[]{:S(2)}, u32[]{:S(2)}) async-start(bf16[8,128,384]{2,1,0:T(8,128)(2,1)} %get-tuple-element.232), calls=%async_computation | async-start | bytes 1572864 | tf_op jit(solution)/shard_map/all_to_all | solution.py:1131
  15.2 3.9 %collective-permute-start.2 = (f32[2,16,512]{2,1,0:T(8,128)}, f32[2,16,512]{2,1,0:T(8,128)S(1)}, u32[]{:S(2)}, u32[]{:S(2)}) collective-permute-start(f32[2,16,512]{2,1,0:T(8,128)} %get-tuple-element.237), channel_id=1, source_target_pairs={{0,1},{1,2},{2,3},{3,4},{4,5},{5,6},{6,7},{8,9},{9,10},{10,11},{11... | collective-permute-start | bytes 196616 | tf_op jit(solution)/shard_map/ppermute | solution.py:896
  27.3 2.0 collective-permute-done.1
  29.9 6.2 %all-to-all-done = bf16[8,128,384]{2,1,0:T(8,128)(2,1)} async-done(((bf16[8,128,384]{2,1,0:T(8,128)(2,1)}), bf16[8,128,384]{2,1,0:T(8,128)(2,1)}, u32[]{:S(2)}, u32[]{:S(2)}) %all-to-all-start) | async-done | bytes 786464 | tf_op jit(solution)/shard_map/all_to_all | solution.py:1131
  36.1 11.8 %shard_map.357 = (bf16[2,1024,1024]{2,1,0:T(8,128)(2,1)}, bf16[8,144,128]{2,1,0:T(8,128)(2,1)}) custom-call(s32[2]{0:T(128)} %limits.1, bf16[1024,384]{1,0:T(8,128)(2,1)} %bitcast.3.content.keys.values, bf16[1024,384]{1,0:T(8,128)(2,1)} %bitcast.3.content.keys.values, bf16[1024,384]{1,0:T(8,128)(2,1)} %bitcast.3.content.keys.values, f32[1,128]{1,0:T(1,128)} %tile.9.shift, ...), custom_call_target="tpu_custom_call" | custom-call | flops 3221225472 | bytes 4194304 | tf_op jit(solution)/shard_map/pallas_call | solution.py:1329
  47.9 3.4 %all-to-all-start.1 = ((bf16[8,144,128]{2,1,0:T(8,128)(2,1)}), bf16[8,144,128]{2,1,0:T(8,128)(2,1)S(1)}, u32[]{:S(2)}, u32[]{:S(2)}) async-start(bf16[8,144,128]{2,1,0:T(8,128)(2,1)} %get-tuple-element.239), calls=%async_computation.1 | async-start | bytes 589824 | tf_op jit(solution)/shard_map/all_to_all | solution.py:1558
  52.6 4.2 %shard_map.358 = (f32[32,512]{1,0:T(8,128)}, f32[32,512]{1,0:T(8,128)}) custom-call(f32[2,16,512]{2,1,0:T(8,128)} %copy-done.26, f32[2,16,512]{2,1,0:T(8,128)} %copy-done.27, bf16[5,512]{1,0:T(8,128)(2,1)} %gains.11, bf16[5,512]{1,0:T(8,128)(2,1)} %biases.7, bf16[2,2048]{1,0:T(2,128)(2,1)} %bias_in.5, bf16[2,512]{1,0:T(2,128)(2,1)} %bias_out.5, ...), custom_call_target="tpu_custom_call" | custom-call | flops 268435456 | bytes 894784 | tf_op jit(solution)/shard_map/pallas_call | solution.py:143
  56.8 3.7 %all-to-all-done.1.blocks = bf16[8,144,128]{2,1,0:T(8,128)(2,1)S(1)} async-done(((bf16[8,144,128]{2,1,0:T(8,128)(2,1)}), bf16[8,144,128]{2,1,0:T(8,128)(2,1)S(1)}, u32[]{:S(2)}, u32[]{:S(2)}) %all-to-all-start.1) | async-done | bytes 294944 | tf_op jit(solution)/shard_map/all_to_all | solution.py:1558
  61.2 4.7 %shard_map.359 = (f32[288,512]{1,0:T(8,128)}, bf16[256,1024]{1,0:T(8,128)(2,1)}, f32[256,512]{1,0:T(8,128)}, f32[256,512]{1,0:T(8,128)}, bf16[288,512]{1,0:T(8,1...) custom-call(s32[4]{0:T(128)} %pad_add_fusion.2.info, bf16[8,144,128]{2,1,0:T(8,128)(2,1)} %copy-done.19, ...), custom_call_target="tpu_custom_call" | custom-call | flops 402653184 | bytes 1342177 | tf_op jit(solution)/shard_map/pallas_call | solution.py:143
  66.0 3.9 %all-to-all-start.2 = ((f32[32,8,128]{2,1,0:T(8,128)}), f32[32,8,128]{2,1,0:T(8,128)S(1)}, u32[]{:S(2)}, u32[]{:S(2)}) async-start(f32[32,8,128]{2,1,0:T(8,128)} %bitcast.55), calls=%async_computation.2 | async-start | bytes 262144 | tf_op jit(solution)/shard_map/all_to_all | solution.py:891
  71.0 6.4 %all-to-all-done.2 = f32[32,8,128]{2,1,0:T(8,128)S(1)} async-done(((f32[32,8,128]{2,1,0:T(8,128)}), f32[32,8,128]{2,1,0:T(8,128)S(1)}, u32[]{:S(2)}, u32[]{:S(2)}) %all-to-all-start.2) | async-done | bytes 131104 | tf_op jit(solution)/shard_map/all_to_all | solution.py:891
  78.1 9.6 %shard_map.360 = (f32[256,512]{1,0:T(8,128)}, f32[256,512]{1,0:T(8,128)}, f32[288,512]{1,0:T(8,128)}, f32[288,512]{1,0:T(8,128)}, bf16[256,6144]{1,0:T(8,128)(2,...) custom-call(s32[8]{0:T(128)} %pad_add_fusion.1.limits, s32[1]{0:T(128)} %bitcast.1.utt_index, ...), custom_call_target="tpu_custom_call" | custom-call | flops 2415919104 | bytes 8053063 | tf_op jit(solution)/shard_map/pallas_call | solution.py:143
  87.9 2.6 all-to-all-start.3
  91.1 2.7 collective-permute-done.4.refs_1_.refs_3_.refs_5_.refs_7_
  93.8 5.9 %shard_map.361 = (bf16[512,512]{1,0:T(8,128)(2,1)}, bf16[512,512]{1,0:T(8,128)(2,1)}, bf16[512,512]{1,0:T(8,128)(2,1)}, bf16[512,512]{1,0:T(8,128)(2,1)}) custom-call(s32[4]{0:T(128)} %add_add_fusion.1.places, bf16[256,6144]{1,0:T(8,128)(2,1)} %get-tuple-element.272.refs_0_.refs_2_.refs_4_.refs_6_, ...), custom_call_target="tpu_custom_call" | custom-call | flops 1400000000 | bytes 4666666 | tf_op jit(solution)/shard_map/pallas_call | solution.py:143
  100.3 5.9 %shard_map.362 = (f32[8,512]{1,0:T(8,128)}, f32[256,512]{1,0:T(8,128)}, bf16[256,1536]{1,0:T(8,128)(2,1)}, bf16[8,128,128]{2,1,0:T(8,128)(2,1)}, f32[16,512]{1,0:T(8,128)}) custom-call(s32[4]{0:T(128)} %pad_add_fusion.2.info, f32[288,512]{1,0:T(8,128)} %get-tuple-element.253.grad_batch, f32[288,512]{1,0:T(8,128)} %get-tuple-element.254.normed_batch, ...), custom_call_target="tpu_custom_call" | custom-call | flops 536870912 | bytes 1789569 | tf_op jit(solution)/shard_map/pallas_call | solution.py:143
  106.7 4.1 %all-to-all-start.4 = ((bf16[8,128,128]{2,1,0:T(8,128)(2,1)}), bf16[8,128,128]{2,1,0:T(8,128)(2,1)}, u32[]{:S(2)}, u32[]{:S(2)}) async-start(bf16[8,128,128]{2,1,0:T(8,128)(2,1)} %get-tuple-element.267), calls=%async_computation.4 | async-start | bytes 524288 | tf_op jit(solution)/shard_map/all_to_all | solution.py:1131
  110.8 1.9 collective-permute-start.7
  114.7 4.4 %shard_map.363 = (bf16[512,512]{1,0:T(8,128)(2,1)}, bf16[512,512]{1,0:T(8,128)(2,1)}) custom-call(s32[4]{0:T(128)} %add_add_fusion.1.places, bf16[256,1024]{1,0:T(8,128)(2,1)} %get-tuple-element.270.refs_0_.refs_8_, bf16[256,1024]{1,0:T(8,128)(2,1)} %collective-permute-done.5.refs_1_.refs_9_, bf16[256,1536]{1,0:T(8,128)(2,1)} %get-tuple-element.271.refs_2_.refs_10_, ...), custom_call_target="tpu_custom_call" | custom-call | flops 700000000 | bytes 2333333 | tf_op jit(solution)/shard_map/pallas_call | solution.py:143
  120.6 12.8 %shard_map.364 = (bf16[1024,384]{1,0:T(8,128)(2,1)}, f32[64,512]{1,0:T(8,128)}, f32[8,128]{1,0:T(8,128)}) custom-call(bf16[2,1024,1024]{2,1,0:T(8,128)(2,1)} %get-tuple-element.252.weights, bf16[1024,384]{1,0:T(8,128)(2,1)} %bitcast.3.content.keys.values, bf16[1024,128]{1,0:T(8,128)(2,1)} %bitcast.22.grads, bf16[1024,384]{1,0:T(8,128)(2,1)} %bitcast.3.content.keys.values, ...), custom_call_target="tpu_custom_call" | custom-call | flops 4294967296 | bytes 4194304 | tf_op jit(solution)/shard_map/pallas_call | solution.py:1369
  133.4 4.2 %all-to-all-start.5 = ((bf16[8,128,384]{2,1,0:T(8,128)(2,1)}), bf16[8,128,384]{2,1,0:T(8,128)(2,1)}, u32[]{:S(2)}, u32[]{:S(2)}) async-start(bf16[8,128,384]{2,1,0:T(8,128)(2,1)} %bitcast.48), calls=%async_computation.5 | async-start | bytes 1572864 | tf_op jit(solution)/shard_map/all_to_all | solution.py:1740
  142.4 4.0 %shard_map.365 = (bf16[256,512]{1,0:T(8,128)(2,1)}, bf16[256,512]{1,0:T(8,128)(2,1)}, bf16[256,512]{1,0:T(8,128)(2,1)}, bf16[256,512]{1,0:T(8,128)(2,1)}, bf16[2...) custom-call(s32[3]{0:T(128)} %pad_add_fusion.3.sides, bf16[512,512]{1,0:T(8,128)(2,1)} %get-tuple-element.283.refs_0_, ...), custom_call_target="tpu_custom_call" | custom-call | bytes 9437184 | tf_op jit(solution)/shard_map/pallas_call | solution.py:785
  150.9 4.3 %shard_map.366 = (bf16[512,512]{1,0:T(8,128)(2,1)}, bf16[1024,512]{1,0:T(8,128)(2,1)}, bf16[512,512]{1,0:T(8,128)(2,1)}, bf16[512,512]{1,0:T(8,128)(2,1)}) custom-call(s32[4]{0:T(128)} %add_add_fusion.1.places, bf16[256,3072]{1,0:T(8,128)(2,1)} %get-tuple-element.295.refs_0_.refs_2_.refs_4_, ...), custom_call_target="tpu_custom_call" | custom-call | tf_op jit(solution)/shard_map/pallas_call | solution.py:143
  155.2 4.9 %collective-permute-done.11.refs_1_ = bf16[256,512]{1,0:T(8,128)(2,1)S(1)} collective-permute-done((bf16[256,512]{1,0:T(8,128)(2,1)}, bf16[256,512]{1,0:T(8,128)(2,1)S(1)}, u32[]{:S(2)}, u32[]{:S(2)}) %collective-permute-start.11) | collective-permute-done | bytes 262176 | tf_op jit(solution)/shard_map/ppermute | solution.py:729
  160.1 7.4 %shard_map.367 = (f32[256,512]{1,0:T(8,128)}, bf16[256,3072]{1,0:T(8,128)(2,1)}, bf16[256,1024]{1,0:T(8,128)(2,1)}, f32[16,512]{1,0:T(8,128)}) custom-call(s32[1]{0:T(128)} %bitcast.16.core, bf16[8,128,384]{2,1,0:T(8,128)(2,1)} %all-to-all-done.5.returned, f32[256,512]{1,0:T(8,128)} %get-tuple-element.302.grad_attend, f32[256,512]{1,0:T(8,128)} %bitcast.47, ...), custom_call_target="tpu_custom_call" | custom-call | flops 1476395008 | bytes 4921316 | tf_op jit(solution)/shard_map/pallas_call | solution.py:143
  167.6 3.7 %collective-permute-done.15.grad_pre_other.grad_low_other.attend_rows_other = bf16[256,3072]{1,0:T(8,128)(2,1)} collective-permute-done((bf16[256,3072]{1,0:T(8,128)(2,1)}, bf16[256,3072]{1,0:T(8,128)(2,1)}, u32[]{:S(2)}, u32[]{:S(2)}) %collective-permute-start.15) | collective-permute-done | bytes 1572896 | tf_op jit(solution)/shard_map/ppermute | solution.py:729
  171.4 5.5 %shard_map.368 = (bf16[512,512]{1,0:T(8,128)(2,1)}, bf16[512,512]{1,0:T(8,128)(2,1)}, bf16[512,512]{1,0:T(8,128)(2,1)}) custom-call(s32[4]{0:T(128)} %add_add_fusion.1.places, bf16[512,512]{1,0:T(8,128)(2,1)} %get-tuple-element.317.hidden_cols, bf16[256,1024]{1,0:T(8,128)(2,1)} %get-tuple-element.318.grad_pre, ...), custom_call_target="tpu_custom_call" | custom-call | flops 805306368 | bytes 6000000 | tf_op jit(solution)/shard_map/pallas_call | solution.py:1011
  176.9 2.0 collective-permute-start.16
  187.9 3.2 %shard_map.369 = (bf16[512,512]{1,0:T(8,128)(2,1)S(1)}, bf16[512,512]{1,0:T(8,128)(2,1)S(1)}, bf16[512,512]{1,0:T(8,128)(2,1)S(1)}) custom-call(s32[4]{0:T(128)S(1)} %copy-done.15, bf16[512,512]{1,0:T(8,128)(2,1)S(1)} %copy-done.2, bf16[256,1024]{1,0:T(8,128)(2,1)S(1)} %copy-done.5, ...), custom_call_target="tpu_custom_call" | custom-call | flops 805306368 | bytes 6000000 | tf_op jit(solution)/shard_map/pallas_call | solution.py:1011
  196.1 2.1 collective-permute-start.35
  204.2 3.3 %collective-permute-start.26 = (bf16[256,512]{1,0:T(8,128)(2,1)S(1)}, bf16[256,512]{1,0:T(8,128)(2,1)S(1)}, u32[]{:S(2)}, u32[]{:S(2)}) collective-permute-start(bf16[256,512]{1,0:T(8,128)(2,1)S(1)} %get-tuple-element.341), channel_id=1, source_target_pairs={{0,4},{1,5},{2,6},{3,7},{4,0},{5,1},{6,2},{7,3},{8,12},{9,13},{10,... | collective-permute-start | bytes 786440 | tf_op jit(solution)/shard_map/ppermute | solution.py:729
  209.9 5.5 %collective-permute-done.18.refs_1_ = bf16[256,512]{1,0:T(8,128)(2,1)S(1)} collective-permute-done((bf16[256,512]{1,0:T(8,128)(2,1)S(1)}, bf16[256,512]{1,0:T(8,128)(2,1)S(1)}, u32[]{:S(2)}, u32[]{:S(2)}) %collective-permute-start.18) | collective-permute-done | bytes 262176 | tf_op jit(solution)/shard_map/ppermute | solution.py:729
  215.5 5.5 %collective-permute-done.26.refs_1_ = bf16[256,512]{1,0:T(8,128)(2,1)S(1)} collective-permute-done((bf16[256,512]{1,0:T(8,128)(2,1)S(1)}, bf16[256,512]{1,0:T(8,128)(2,1)S(1)}, u32[]{:S(2)}, u32[]{:S(2)}) %collective-permute-start.26) | collective-permute-done | bytes 262176 | tf_op jit(solution)/shard_map/ppermute | solution.py:729
  221.3 2.1 collective-permute-start.39
  226.5 4.8 %collective-permute-done.38.refs_1_ = bf16[128,512]{1,0:T(8,128)(2,1)S(1)} collective-permute-done((bf16[128,512]{1,0:T(8,128)(2,1)S(1)}, bf16[128,512]{1,0:T(8,128)(2,1)S(1)}, u32[]{:S(2)}, u32[]{:S(2)}) %collective-permute-start.38) | collective-permute-done | bytes 131104 | tf_op jit(solution)/shard_map/ppermute | solution.py:729
  231.5 4.0 %collective-permute-done.20.refs_1_ = bf16[128,512]{1,0:T(8,128)(2,1)S(1)} collective-permute-done((bf16[128,512]{1,0:T(8,128)(2,1)S(1)}, bf16[128,512]{1,0:T(8,128)(2,1)S(1)}, u32[]{:S(2)}, u32[]{:S(2)}) %collective-permute-start.20) | collective-permute-done | bytes 131104 | tf_op jit(solution)/shard_map/ppermute | solution.py:729
  235.5 4.2 %collective-permute-start.21 = (bf16[256,512]{1,0:T(8,128)(2,1)S(1)}, bf16[256,512]{1,0:T(8,128)(2,1)S(1)}, u32[]{:S(2)}, u32[]{:S(2)}) collective-permute-start(bf16[256,512]{1,0:T(8,128)(2,1)S(1)} %shard_map.374.refs_0_), channel_id=1, source_target_pairs={{0,2},{1,3},{2,0},{3,1},{4,6},{5,7},{6,4},{7,5},{8,10},{9,11},{10,... | collective-permute-start | bytes 786440 | tf_op jit(solution)/shard_map/ppermute | solution.py:729
  239.8 2.2 collective-permute-start.29
  243.0 7.7 %collective-permute-done.21.refs_1_ = bf16[256,512]{1,0:T(8,128)(2,1)S(1)} collective-permute-done((bf16[256,512]{1,0:T(8,128)(2,1)S(1)}, bf16[256,512]{1,0:T(8,128)(2,1)S(1)}, u32[]{:S(2)}, u32[]{:S(2)}) %collective-permute-start.21) | collective-permute-done | bytes 262176 | tf_op jit(solution)/shard_map/ppermute | solution.py:729
  251.8 3.0 collective-permute-done.29.refs_1_
  255.1 9.5 %collective-permute-done.22.refs_1_ = bf16[512,512]{1,0:T(8,128)(2,1)S(1)} collective-permute-done((bf16[512,512]{1,0:T(8,128)(2,1)S(1)}, bf16[512,512]{1,0:T(8,128)(2,1)S(1)}, u32[]{:S(2)}, u32[]{:S(2)}) %collective-permute-start.22) | collective-permute-done | bytes 524320 | tf_op jit(solution)/shard_map/ppermute | solution.py:729
  265.7 2.4 collective-permute-done.30.refs_1_
  276.6 4.8 %shard_map.391 = (f32[2,512,2048]{2,1,0:T(8,128)}, f32[2,2048,512]{2,1,0:T(8,128)}, f32[512,1024]{1,0:T(8,128)}, f32[512,512]{1,0:T(8,128)}, f32[512,512]{1,0:T(8,128)}, /*index=5*/f32[4,512,512]{2,1,0:T(8,128)}) custom-call(s32[4]{0:T(128)} %add_add_fusion.1.places, bf16[1024,512]{1,0:T(8,128)(2,1)} %shard_map.376.refs_0_, ...), custom_call_target="tpu_custom_call" | custom-call | bytes 9437184 | tf_op jit(solution)/shard_map/pallas_call | solution.py:1096
  283.7 4.9 %shard_map.392 = (f32[2,512,2048]{2,1,0:T(8,128)}, f32[2,2048,512]{2,1,0:T(8,128)}, f32[512,1024]{1,0:T(8,128)}, f32[512,512]{1,0:T(8,128)}, f32[512,512]{1,0:T(8,128)}, /*index=5*/f32[4,512,512]{2,1,0:T(8,128)}) custom-call(s32[4]{0:T(128)} %add_add_fusion.2.places, ...), custom_call_target="tpu_custom_call", output_to_operand_aliasing={{0}: (7, {}), {1}: (8, {}), {2}: (9, {}), {3}: (10, {}), {4... | custom-call | bytes 9437184 | tf_op jit(solution)/shard_map/pallas_call | solution.py:1096
  288.6 8.1 %collective-permute-done.47.refs_2_.refs_3_.refs_4_.refs_5_ = bf16[1024,512]{1,0:T(8,128)(2,1)} collective-permute-done((bf16[1024,512]{1,0:T(8,128)(2,1)}, bf16[1024,512]{1,0:T(8,128)(2,1)}, u32[]{:S(2)}, u32[]{:S(2)}) %collective-permute-start.47) | collective-permute-done | bytes 1048608 | tf_op jit(solution)/shard_map/ppermute | solution.py:729
  300.0 4.8 %shard_map.394 = (f32[2,512,2048]{2,1,0:T(8,128)}, f32[2,2048,512]{2,1,0:T(8,128)}, f32[512,1024]{1,0:T(8,128)}, f32[512,512]{1,0:T(8,128)}, f32[512,512]{1,0:T(8,128)}, /*index=5*/f32[4,512,512]{2,1,0:T(8,128)}) custom-call(s32[4]{0:T(128)} %get-tuple-element.450.places, ...), custom_call_target="tpu_custom_call", output_to_operand_aliasing={{0}: (7, {}), {1}: (8, {}), {2}: (9, {}), {3}: (10, {}), {4... | custom-call | bytes 9437184 | tf_op jit(solution)/shard_map/pallas_call | solution.py:1096
  304.9 4.9 %shard_map.395 = (f32[2,512,2048]{2,1,0:T(8,128)}, f32[2,2048,512]{2,1,0:T(8,128)}, f32[512,1024]{1,0:T(8,128)}, f32[512,512]{1,0:T(8,128)}, f32[512,512]{1,0:T(8,128)}, /*index=5*/f32[4,512,512]{2,1,0:T(8,128)}) custom-call(s32[4]{0:T(128)} %get-tuple-element.451.places, ...), custom_call_target="tpu_custom_call", output_to_operand_aliasing={{0}: (7, {}), {1}: (8, {}), {2}: (9, {}), {3}: (10, {}), {4... | custom-call | bytes 9437184 | tf_op jit(solution)/shard_map/pallas_call | solution.py:1096
  (218 shorter events, 70.8 us)
Async XLA Ops:
  7.8 28.2 %all-to-all-start = ((bf16[8,128,384]{2,1,0:T(8,128)(2,1)}), bf16[8,128,384]{2,1,0:T(8,128)(2,1)}, u32[]{:S(2)}, u32[]{:S(2)}) async-start(bf16[8,128,384]{2,1,0:T(8,128)(2,1)} %get-tuple-element.232), calls=%async_computation | async-start | bytes 1572864 | tf_op jit(solution)/shard_map/all_to_all | solution.py:1131
  15.1 10.6 %collective-permute-start = (s32[2]{0:T(128)S(1)}, s32[2]{0:T(128)S(1)}, u32[]{:S(2)}, u32[]{:S(2)}) collective-permute-start(s32[2]{0:T(128)S(1)} %copy-done.30), channel_id=1, source_target_pairs={{0,8},{8,0},{16,24},{24,16},{1,9},{9,1},{17,25},{25,17},{2,10},{10... | collective-permute-start | bytes 32 | tf_op jit(solution)/shard_map/ppermute | solution.py:729
  15.2 32.7 %collective-permute-start.2 = (f32[2,16,512]{2,1,0:T(8,128)}, f32[2,16,512]{2,1,0:T(8,128)S(1)}, u32[]{:S(2)}, u32[]{:S(2)}) collective-permute-start(f32[2,16,512]{2,1,0:T(8,128)} %get-tuple-element.237), channel_id=1, source_target_pairs={{0,1},{1,2},{2,3},{3,4},{4,5},{5,6},{6,7},{8,9},{9,10},{10,11},{11... | collective-permute-start | bytes 196616 | tf_op jit(solution)/shard_map/ppermute | solution.py:896
  19.0 28.9 %collective-permute-start.3 = (f32[2,16,512]{2,1,0:T(8,128)}, f32[2,16,512]{2,1,0:T(8,128)S(1)}, u32[]{:S(2)}, u32[]{:S(2)}) collective-permute-start(f32[2,16,512]{2,1,0:T(8,128)} %get-tuple-element.238), channel_id=1, source_target_pairs={{1,0},{2,1},{3,2},{4,3},{5,4},{6,5},{7,6},{9,8},{10,9},{11,10},{12... | collective-permute-start | bytes 196616 | tf_op jit(solution)/shard_map/ppermute | solution.py:897
  47.9 12.6 %all-to-all-start.1 = ((bf16[8,144,128]{2,1,0:T(8,128)(2,1)}), bf16[8,144,128]{2,1,0:T(8,128)(2,1)S(1)}, u32[]{:S(2)}, u32[]{:S(2)}) async-start(bf16[8,144,128]{2,1,0:T(8,128)(2,1)} %get-tuple-element.239), calls=%async_computation.1 | async-start | bytes 589824 | tf_op jit(solution)/shard_map/all_to_all | solution.py:1558
  66.0 11.4 %all-to-all-start.2 = ((f32[32,8,128]{2,1,0:T(8,128)}), f32[32,8,128]{2,1,0:T(8,128)S(1)}, u32[]{:S(2)}, u32[]{:S(2)}) async-start(f32[32,8,128]{2,1,0:T(8,128)} %bitcast.55), calls=%async_computation.2 | async-start | bytes 262144 | tf_op jit(solution)/shard_map/all_to_all | solution.py:891
  87.9 11.8 %all-to-all-start.3 = ((f32[32,8,128]{2,1,0:T(8,128)}), f32[32,8,128]{2,1,0:T(8,128)S(1)}, u32[]{:S(2)}, u32[]{:S(2)}) async-start(f32[32,8,128]{2,1,0:T(8,128)} %bitcast.54), calls=%async_computation.3 | async-start | bytes 262144 | tf_op jit(solution)/shard_map/all_to_all | solution.py:891
  106.2 7.5 %collective-permute-start.6 = (bf16[256,1536]{1,0:T(8,128)(2,1)}, bf16[256,1536]{1,0:T(8,128)(2,1)S(1)}, u32[]{:S(2)}, u32[]{:S(2)}) collective-permute-start(bf16[256,1536]{1,0:T(8,128)(2,1)} %get-tuple-element.271.refs_2_.refs_10_), channel_id=1, source_target_pairs={{0,8},{8,0},{16,24},{24,16},{1,9},{9,1},{17,25},{25,17},{2,10},{10... | collective-permute-start | bytes 2359304 | tf_op jit(solution)/shard_map/ppermute | solution.py:729
  106.7 13.8 %all-to-all-start.4 = ((bf16[8,128,128]{2,1,0:T(8,128)(2,1)}), bf16[8,128,128]{2,1,0:T(8,128)(2,1)}, u32[]{:S(2)}, u32[]{:S(2)}) async-start(bf16[8,128,128]{2,1,0:T(8,128)(2,1)} %get-tuple-element.267), calls=%async_computation.4 | async-start | bytes 524288 | tf_op jit(solution)/shard_map/all_to_all | solution.py:1131
  110.8 22.6 %collective-permute-start.7 = (bf16[512,512]{1,0:T(8,128)(2,1)}, bf16[512,512]{1,0:T(8,128)(2,1)}, u32[]{:S(2)}, u32[]{:S(2)}) collective-permute-start(bf16[512,512]{1,0:T(8,128)(2,1)} %get-tuple-element.279), channel_id=1, source_target_pairs={{0,1},{1,0},{2,3},{3,2},{4,5},{5,4},{6,7},{7,6},{8,9},{9,8},{10,11... | collective-permute-start | bytes 1572872 | tf_op jit(solution)/shard_map/ppermute | solution.py:729
  112.7 20.7 %collective-permute-start.8 = (bf16[512,512]{1,0:T(8,128)(2,1)}, bf16[512,512]{1,0:T(8,128)(2,1)}, u32[]{:S(2)}, u32[]{:S(2)}) collective-permute-start(bf16[512,512]{1,0:T(8,128)(2,1)} %get-tuple-element.280), channel_id=1, source_target_pairs={{0,16},{8,24},{16,0},{24,8},{1,17},{9,25},{17,1},{25,9},{2,18},{10... | collective-permute-start | bytes 1572872 | tf_op jit(solution)/shard_map/ppermute | solution.py:729
  119.1 14.3 %collective-permute-start.9 = (bf16[512,512]{1,0:T(8,128)(2,1)}, bf16[512,512]{1,0:T(8,128)(2,1)S(1)}, u32[]{:S(2)}, u32[]{:S(2)}) collective-permute-start(bf16[512,512]{1,0:T(8,128)(2,1)} %get-tuple-element.281), channel_id=1, source_target_pairs={{0,2},{1,3},{2,0},{3,1},{4,6},{5,7},{6,4},{7,5},{8,10},{9,11},{10,... | collective-permute-start | bytes 1572872 | tf_op jit(solution)/shard_map/ppermute | solution.py:729
  120.5 30.3 %collective-permute-start.13 = (bf16[256,3072]{1,0:T(8,128)(2,1)}, bf16[256,3072]{1,0:T(8,128)(2,1)}, u32[]{:S(2)}, u32[]{:S(2)}) collective-permute-start(bf16[256,3072]{1,0:T(8,128)(2,1)} %get-tuple-element.295.refs_0_.refs_2_.refs_4_), channel_id=1, source_target_pairs={{0,8},{8,0},{16,24},{24,16},{1,9},{9,1},{17,25},{25,17},{2,10},{10... | collective-permute-start | bytes 4718600 | tf_op jit(solution)/shard_map/ppermute | solution.py:729
  133.4 26.6 %all-to-all-start.5 = ((bf16[8,128,384]{2,1,0:T(8,128)(2,1)}), bf16[8,128,384]{2,1,0:T(8,128)(2,1)}, u32[]{:S(2)}, u32[]{:S(2)}) async-start(bf16[8,128,384]{2,1,0:T(8,128)(2,1)} %bitcast.48), calls=%async_computation.5 | async-start | bytes 1572864 | tf_op jit(solution)/shard_map/all_to_all | solution.py:1740
  141.3 9.6 %collective-permute-start.14 = (bf16[512,512]{1,0:T(8,128)(2,1)}, bf16[512,512]{1,0:T(8,128)(2,1)}, u32[]{:S(2)}, u32[]{:S(2)}) collective-permute-start(bf16[512,512]{1,0:T(8,128)(2,1)} %dynamic_update_slice.6.refs_6_), channel_id=1, source_target_pairs={{0,8},{8,0},{16,24},{24,16},{1,9},{9,1},{17,25},{25,17},{2,10},{10... | collective-permute-start | bytes 1572872 | tf_op jit(solution)/shard_map/ppermute | solution.py:729
  146.4 8.8 %collective-permute-start.10 = (bf16[256,512]{1,0:T(8,128)(2,1)}, bf16[256,512]{1,0:T(8,128)(2,1)S(1)}, u32[]{:S(2)}, u32[]{:S(2)}) collective-permute-start(bf16[256,512]{1,0:T(8,128)(2,1)} %get-tuple-element.292), channel_id=1, source_target_pairs={{0,16},{8,24},{16,0},{24,8},{1,17},{9,25},{17,1},{25,9},{2,18},{10... | collective-permute-start | bytes 786440 | tf_op jit(solution)/shard_map/ppermute | solution.py:729
  147.4 12.7 %collective-permute-start.11 = (bf16[256,512]{1,0:T(8,128)(2,1)}, bf16[256,512]{1,0:T(8,128)(2,1)S(1)}, u32[]{:S(2)}, u32[]{:S(2)}) collective-permute-start(bf16[256,512]{1,0:T(8,128)(2,1)} %get-tuple-element.293), channel_id=1, source_target_pairs={{0,2},{1,3},{2,0},{3,1},{4,6},{5,7},{6,4},{7,5},{8,10},{9,11},{10,... | collective-permute-start | bytes 786440 | tf_op jit(solution)/shard_map/ppermute | solution.py:729
  149.0 11.1 %collective-permute-start.12 = (bf16[256,512]{1,0:T(8,128)(2,1)}, bf16[256,512]{1,0:T(8,128)(2,1)S(1)}, u32[]{:S(2)}, u32[]{:S(2)}) collective-permute-start(bf16[256,512]{1,0:T(8,128)(2,1)} %get-tuple-element.294), channel_id=1, source_target_pairs={{0,1},{1,0},{2,3},{3,2},{4,5},{5,4},{6,7},{7,6},{8,9},{9,8},{10,11... | collective-permute-start | bytes 786440 | tf_op jit(solution)/shard_map/ppermute | solution.py:729
  176.9 14.2 %collective-permute-start.16 = (bf16[512,512]{1,0:T(8,128)(2,1)}, bf16[512,512]{1,0:T(8,128)(2,1)S(1)}, u32[]{:S(2)}, u32[]{:S(2)}) collective-permute-start(bf16[512,512]{1,0:T(8,128)(2,1)} %get-tuple-element.325), channel_id=1, source_target_pairs={{0,1},{1,0},{2,3},{3,2},{4,5},{5,4},{6,7},{7,6},{8,9},{9,8},{10,11... | collective-permute-start | bytes 1572872 | tf_op jit(solution)/shard_map/ppermute | solution.py:729
  178.8 14.0 %collective-permute-start.24 = (bf16[512,512]{1,0:T(8,128)(2,1)}, bf16[512,512]{1,0:T(8,128)(2,1)S(1)}, u32[]{:S(2)}, u32[]{:S(2)}) collective-permute-start(bf16[512,512]{1,0:T(8,128)(2,1)} %get-tuple-element.335), channel_id=1, source_target_pairs={{0,16},{8,24},{16,0},{24,8},{1,17},{9,25},{17,1},{25,9},{2,18},{10... | collective-permute-start | bytes 1572872 | tf_op jit(solution)/shard_map/ppermute | solution.py:729
  179.9 15.7 %collective-permute-start.32 = (bf16[512,512]{1,0:T(8,128)(2,1)}, bf16[512,512]{1,0:T(8,128)(2,1)S(1)}, u32[]{:S(2)}, u32[]{:S(2)}) collective-permute-start(bf16[512,512]{1,0:T(8,128)(2,1)} %get-tuple-element.352), channel_id=1, source_target_pairs={{0,2},{1,3},{2,0},{3,1},{4,6},{5,7},{6,4},{7,5},{8,10},{9,11},{10,... | collective-permute-start | bytes 1572872 | tf_op jit(solution)/shard_map/ppermute | solution.py:729
  180.3 15.3 %collective-permute-start.33 = (f32[56,512]{1,0:T(8,128)S(1)}, f32[56,512]{1,0:T(8,128)S(1)}, u32[]{:S(2)}, u32[]{:S(2)}) collective-permute-start(f32[56,512]{1,0:T(8,128)S(1)} %pad_maximum_fusion.1), channel_id=1, source_target_pairs={{0,4},{1,5},{2,6},{3,7},{4,0},{5,1},{6,2},{7,3},{8,12},{9,13},{10,... | collective-permute-start | bytes 344072 | tf_op jit(solution)/shard_map/ppermute | solution.py:729
  191.9 7.8 %collective-permute-start.17 = (bf16[256,512]{1,0:T(8,128)(2,1)}, bf16[256,512]{1,0:T(8,128)(2,1)}, u32[]{:S(2)}, u32[]{:S(2)}) collective-permute-start(bf16[256,512]{1,0:T(8,128)(2,1)} %get-tuple-element.327), channel_id=1, source_target_pairs={{0,16},{8,24},{16,0},{24,8},{1,17},{9,25},{17,1},{25,9},{2,18},{10... | collective-permute-start | bytes 786440 | tf_op jit(solution)/shard_map/ppermute | solution.py:729
  193.6 10.5 %collective-permute-start.25 = (bf16[256,512]{1,0:T(8,128)(2,1)}, bf16[256,512]{1,0:T(8,128)(2,1)S(1)}, u32[]{:S(2)}, u32[]{:S(2)}) collective-permute-start(bf16[256,512]{1,0:T(8,128)(2,1)} %get-tuple-element.338), channel_id=1, source_target_pairs={{0,2},{1,3},{2,0},{3,1},{4,6},{5,7},{6,4},{7,5},{8,10},{9,11},{10,... | collective-permute-start | bytes 786440 | tf_op jit(solution)/shard_map/ppermute | solution.py:729
  195.7 11.8 %collective-permute-start.34 = (bf16[256,512]{1,0:T(8,128)(2,1)S(1)}, bf16[256,512]{1,0:T(8,128)(2,1)S(1)}, u32[]{:S(2)}, u32[]{:S(2)}) collective-permute-start(bf16[256,512]{1,0:T(8,128)(2,1)S(1)} %get-tuple-element.360), channel_id=1, source_target_pairs={{0,1},{1,0},{2,3},{3,2},{4,5},{5,4},{6,7},{7,6},{8,9},{9,8},{10,11... | collective-permute-start | bytes 786440 | tf_op jit(solution)/shard_map/ppermute | solution.py:729
  196.1 11.5 %collective-permute-start.35 = (f32[56,512]{1,0:T(8,128)S(1)}, f32[56,512]{1,0:T(8,128)S(1)}, u32[]{:S(2)}, u32[]{:S(2)}) collective-permute-start(f32[56,512]{1,0:T(8,128)S(1)} %fusion), channel_id=1, source_target_pairs={{0,2},{1,3},{2,0},{3,1},{4,6},{5,7},{6,4},{7,5},{8,10},{9,11},{10,... | collective-permute-start | bytes 344072 | tf_op jit(solution)/shard_map/ppermute | solution.py:729
  203.6 11.8 %collective-permute-start.18 = (bf16[256,512]{1,0:T(8,128)(2,1)S(1)}, bf16[256,512]{1,0:T(8,128)(2,1)S(1)}, u32[]{:S(2)}, u32[]{:S(2)}) collective-permute-start(bf16[256,512]{1,0:T(8,128)(2,1)S(1)} %get-tuple-element.329), channel_id=1, source_target_pairs={{0,2},{1,3},{2,0},{3,1},{4,6},{5,7},{6,4},{7,5},{8,10},{9,11},{10,... | collective-permute-start | bytes 786440 | tf_op jit(solution)/shard_map/ppermute | solution.py:729
  204.2 16.7 %collective-permute-start.26 = (bf16[256,512]{1,0:T(8,128)(2,1)S(1)}, bf16[256,512]{1,0:T(8,128)(2,1)S(1)}, u32[]{:S(2)}, u32[]{:S(2)}) collective-permute-start(bf16[256,512]{1,0:T(8,128)(2,1)S(1)} %get-tuple-element.341), channel_id=1, source_target_pairs={{0,4},{1,5},{2,6},{3,7},{4,0},{5,1},{6,2},{7,3},{8,12},{9,13},{10,... | collective-permute-start | bytes 786440 | tf_op jit(solution)/shard_map/ppermute | solution.py:729
  207.7 13.4 %collective-permute-start.36 = (bf16[256,512]{1,0:T(8,128)(2,1)S(1)}, bf16[256,512]{1,0:T(8,128)(2,1)S(1)}, u32[]{:S(2)}, u32[]{:S(2)}) collective-permute-start(bf16[256,512]{1,0:T(8,128)(2,1)S(1)} %get-tuple-element.365), channel_id=1, source_target_pairs={{0,16},{8,24},{16,0},{24,8},{1,17},{9,25},{17,1},{25,9},{2,18},{10... | collective-permute-start | bytes 786440 | tf_op jit(solution)/shard_map/ppermute | solution.py:729
  208.7 12.4 %collective-permute-start.37 = (f32[56,512]{1,0:T(8,128)S(1)}, f32[56,512]{1,0:T(8,128)S(1)}, u32[]{:S(2)}, u32[]{:S(2)}) collective-permute-start(f32[56,512]{1,0:T(8,128)S(1)} %add.99), channel_id=1, source_target_pairs={{0,16},{8,24},{16,0},{24,8},{1,17},{9,25},{17,1},{25,9},{2,18},{10... | collective-permute-start | bytes 344072 | tf_op jit(solution)/shard_map/ppermute | solution.py:729
  215.4 9.8 %collective-permute-start.19 = (bf16[128,512]{1,0:T(8,128)(2,1)S(1)}, bf16[128,512]{1,0:T(8,128)(2,1)S(1)}, u32[]{:S(2)}, u32[]{:S(2)}) collective-permute-start(bf16[128,512]{1,0:T(8,128)(2,1)S(1)} %get-tuple-element.331), channel_id=1, source_target_pairs={{0,4},{1,5},{2,6},{3,7},{4,0},{5,1},{6,2},{7,3},{8,12},{9,13},{10,... | collective-permute-start | bytes 393224 | tf_op jit(solution)/shard_map/ppermute | solution.py:729
  221.2 10.1 %collective-permute-start.38 = (bf16[128,512]{1,0:T(8,128)(2,1)S(1)}, bf16[128,512]{1,0:T(8,128)(2,1)S(1)}, u32[]{:S(2)}, u32[]{:S(2)}) collective-permute-start(bf16[128,512]{1,0:T(8,128)(2,1)S(1)} %get-tuple-element.370), channel_id=1, source_target_pairs={{0,4},{1,5},{2,6},{3,7},{4,0},{5,1},{6,2},{7,3},{8,12},{9,13},{10,... | collective-permute-start | bytes 393224 | tf_op jit(solution)/shard_map/ppermute | solution.py:729
  221.3 10.0 %collective-permute-start.39 = (f32[56,512]{1,0:T(8,128)S(1)}, f32[56,512]{1,0:T(8,128)S(1)}, u32[]{:S(2)}, u32[]{:S(2)}) collective-permute-start(f32[56,512]{1,0:T(8,128)S(1)} %add.100), channel_id=1, source_target_pairs={{0,1},{1,0},{2,3},{3,2},{4,5},{5,4},{6,7},{7,6},{8,9},{9,8},{10,11... | collective-permute-start | bytes 344072 | tf_op jit(solution)/shard_map/ppermute | solution.py:729
  225.2 10.3 %collective-permute-start.20 = (bf16[128,512]{1,0:T(8,128)(2,1)S(1)}, bf16[128,512]{1,0:T(8,128)(2,1)S(1)}, u32[]{:S(2)}, u32[]{:S(2)}) collective-permute-start(bf16[128,512]{1,0:T(8,128)(2,1)S(1)} %shard_map.373.refs_0_), channel_id=1, source_target_pairs={{0,4},{1,5},{2,6},{3,7},{4,0},{5,1},{6,2},{7,3},{8,12},{9,13},{10,... | collective-permute-start | bytes 393224 | tf_op jit(solution)/shard_map/ppermute | solution.py:729
  226.4 13.3 %collective-permute-start.28 = (bf16[128,512]{1,0:T(8,128)(2,1)S(1)}, bf16[128,512]{1,0:T(8,128)(2,1)S(1)}, u32[]{:S(2)}, u32[]{:S(2)}) collective-permute-start(bf16[128,512]{1,0:T(8,128)(2,1)S(1)} %shard_map.380.refs_0_), channel_id=1, source_target_pairs={{0,1},{1,0},{2,3},{3,2},{4,5},{5,4},{6,7},{7,6},{8,9},{9,8},{10,11... | collective-permute-start | bytes 393224 | tf_op jit(solution)/shard_map/ppermute | solution.py:729
  231.3 10.7 %collective-permute-start.40 = (bf16[128,512]{1,0:T(8,128)(2,1)S(1)}, bf16[128,512]{1,0:T(8,128)(2,1)S(1)}, u32[]{:S(2)}, u32[]{:S(2)}) collective-permute-start(bf16[128,512]{1,0:T(8,128)(2,1)S(1)} %shard_map.387.refs_0_), channel_id=1, source_target_pairs={{0,4},{1,5},{2,6},{3,7},{4,0},{5,1},{6,2},{7,3},{8,12},{9,13},{10,... | collective-permute-start | bytes 393224 | tf_op jit(solution)/shard_map/ppermute | solution.py:729
  231.4 10.6 %collective-permute-start.41 = (f32[56,512]{1,0:T(8,128)S(1)}, f32[56,512]{1,0:T(8,128)S(1)}, u32[]{:S(2)}, u32[]{:S(2)}) collective-permute-start(f32[56,512]{1,0:T(8,128)S(1)} %add.101), channel_id=1, source_target_pairs={{0,8},{8,0},{16,24},{24,16},{1,9},{9,1},{17,25},{25,17},{2,10},{10... | collective-permute-start | bytes 344072 | tf_op jit(solution)/shard_map/ppermute | solution.py:729
  235.5 15.3 %collective-permute-start.21 = (bf16[256,512]{1,0:T(8,128)(2,1)S(1)}, bf16[256,512]{1,0:T(8,128)(2,1)S(1)}, u32[]{:S(2)}, u32[]{:S(2)}) collective-permute-start(bf16[256,512]{1,0:T(8,128)(2,1)S(1)} %shard_map.374.refs_0_), channel_id=1, source_target_pairs={{0,2},{1,3},{2,0},{3,1},{4,6},{5,7},{6,4},{7,5},{8,10},{9,11},{10,... | collective-permute-start | bytes 786440 | tf_op jit(solution)/shard_map/ppermute | solution.py:729
  239.8 15.0 %collective-permute-start.29 = (bf16[256,512]{1,0:T(8,128)(2,1)S(1)}, bf16[256,512]{1,0:T(8,128)(2,1)S(1)}, u32[]{:S(2)}, u32[]{:S(2)}) collective-permute-start(bf16[256,512]{1,0:T(8,128)(2,1)S(1)} %shard_map.381.refs_0_), channel_id=1, source_target_pairs={{0,4},{1,5},{2,6},{3,7},{4,0},{5,1},{6,2},{7,3},{8,12},{9,13},{10,... | collective-permute-start | bytes 786440 | tf_op jit(solution)/shard_map/ppermute | solution.py:729
  242.0 12.9 %collective-permute-start.42 = (bf16[256,512]{1,0:T(8,128)(2,1)S(1)}, bf16[256,512]{1,0:T(8,128)(2,1)S(1)}, u32[]{:S(2)}, u32[]{:S(2)}) collective-permute-start(bf16[256,512]{1,0:T(8,128)(2,1)S(1)} %shard_map.388.refs_0_), channel_id=1, source_target_pairs={{0,16},{8,24},{16,0},{24,8},{1,17},{9,25},{17,1},{25,9},{2,18},{10... | collective-permute-start | bytes 786440 | tf_op jit(solution)/shard_map/ppermute | solution.py:729
  250.8 13.8 %collective-permute-start.22 = (bf16[512,512]{1,0:T(8,128)(2,1)S(1)}, bf16[512,512]{1,0:T(8,128)(2,1)S(1)}, u32[]{:S(2)}, u32[]{:S(2)}) collective-permute-start(bf16[512,512]{1,0:T(8,128)(2,1)S(1)} %shard_map.375.refs_0_), channel_id=1, source_target_pairs={{0,16},{8,24},{16,0},{24,8},{1,17},{9,25},{17,1},{25,9},{2,18},{10... | collective-permute-start | bytes 1572872 | tf_op jit(solution)/shard_map/ppermute | solution.py:729
  254.9 13.3 %collective-permute-start.30 = (bf16[512,512]{1,0:T(8,128)(2,1)S(1)}, bf16[512,512]{1,0:T(8,128)(2,1)S(1)}, u32[]{:S(2)}, u32[]{:S(2)}) collective-permute-start(bf16[512,512]{1,0:T(8,128)(2,1)S(1)} %shard_map.382.refs_0_), channel_id=1, source_target_pairs={{0,2},{1,3},{2,0},{3,1},{4,6},{5,7},{6,4},{7,5},{8,10},{9,11},{10,... | collective-permute-start | bytes 1572872 | tf_op jit(solution)/shard_map/ppermute | solution.py:729
  255.0 14.2 %collective-permute-start.43 = (bf16[512,512]{1,0:T(8,128)(2,1)S(1)}, bf16[512,512]{1,0:T(8,128)(2,1)S(1)}, u32[]{:S(2)}, u32[]{:S(2)}) collective-permute-start(bf16[512,512]{1,0:T(8,128)(2,1)S(1)} %shard_map.389.refs_0_), channel_id=1, source_target_pairs={{0,1},{1,0},{2,3},{3,2},{4,5},{5,4},{6,7},{7,6},{8,9},{9,8},{10,11... | collective-permute-start | bytes 1572872 | tf_op jit(solution)/shard_map/ppermute | solution.py:729
  270.3 13.4 %collective-permute-start.31 = (bf16[1024,512]{1,0:T(8,128)(2,1)}, bf16[1024,512]{1,0:T(8,128)(2,1)}, u32[]{:S(2)}, u32[]{:S(2)}) collective-permute-start(bf16[1024,512]{1,0:T(8,128)(2,1)} %shard_map.383.refs_1_), channel_id=1, source_target_pairs={{0,8},{8,0},{16,24},{24,16},{1,9},{9,1},{17,25},{25,17},{2,10},{10... | collective-permute-start | bytes 3145736 | tf_op jit(solution)/shard_map/ppermute | solution.py:729
  270.8 12.9 %collective-permute-start.23 = (bf16[1024,512]{1,0:T(8,128)(2,1)}, bf16[1024,512]{1,0:T(8,128)(2,1)}, u32[]{:S(2)}, u32[]{:S(2)}) collective-permute-start(bf16[1024,512]{1,0:T(8,128)(2,1)} %shard_map.376.refs_0_), channel_id=1, source_target_pairs={{0,8},{8,0},{16,24},{24,16},{1,9},{9,1},{17,25},{25,17},{2,10},{10... | collective-permute-start | bytes 3145736 | tf_op jit(solution)/shard_map/ppermute | solution.py:729
  270.8 25.9 %collective-permute-start.47 = (bf16[1024,512]{1,0:T(8,128)(2,1)}, bf16[1024,512]{1,0:T(8,128)(2,1)}, u32[]{:S(2)}, u32[]{:S(2)}) collective-permute-start(bf16[1024,512]{1,0:T(8,128)(2,1)} %shard_map.390.refs_2_.refs_3_.refs_4_.refs_5_), channel_id=1, source_target_pairs={{0,2},{1,3},{2,0},{3,1},{4,6},{5,7},{6,4},{7,5},{8,10},{9,11},{10,... | collective-permute-start | bytes 3145736 | tf_op jit(solution)/shard_map/ppermute | solution.py:729
  271.6 25.6 %collective-permute-start.46 = (bf16[1024,512]{1,0:T(8,128)(2,1)}, bf16[1024,512]{1,0:T(8,128)(2,1)}, u32[]{:S(2)}, u32[]{:S(2)}) collective-permute-start(bf16[1024,512]{1,0:T(8,128)(2,1)} %shard_map.383.refs_1_), channel_id=1, source_target_pairs={{0,16},{8,24},{16,0},{24,8},{1,17},{9,25},{17,1},{25,9},{2,18},{10... | collective-permute-start | bytes 3145736 | tf_op jit(solution)/shard_map/ppermute | solution.py:729
  273.3 25.5 %collective-permute-start.45 = (bf16[1024,512]{1,0:T(8,128)(2,1)}, bf16[1024,512]{1,0:T(8,128)(2,1)}, u32[]{:S(2)}, u32[]{:S(2)}) collective-permute-start(bf16[1024,512]{1,0:T(8,128)(2,1)} %shard_map.376.refs_0_), channel_id=1, source_target_pairs={{0,1},{1,0},{2,3},{3,2},{4,5},{5,4},{6,7},{7,6},{8,9},{9,8},{10,11... | collective-permute-start | bytes 3145736 | tf_op jit(solution)/shard_map/ppermute | solution.py:729
  (44 other events, 303.8 us)
